TPU v7x, 512 devices: a whole 4x8x8 slice. The times are simulated.
512 devices in a mesh: gx: 32 (over x, z), gy: 16 (over y, core).
Axes of the slice: x: 4, y: 8, z: 8, core: 2. Of those that a mesh axis runs over, the one named last changes fastest.
Arguments:
- rhs: float32 [512, 512, 128], P('gx', 'gy'), may hold values from -6 to 6
- target: float32 [512, 512, 128], P('gx', 'gy'), may hold values from -6 to 6
- stencils: float32 [9, 27], replicated, may hold values from -0.006 to 0.11, as said below
- face_mask: int32 [6], replicated, may hold values 0 or 1
Outputs:
- solution: float32 [512, 512, 128], P('gx', 'gy')
- grad_rhs: float32 [512, 512, 128], P('gx', 'gy')
- grad_stencils: float32 [9, 27], replicated
Inputs may be any that keep to these rules, and one draw needn't show every extreme that they name: `stencils`: entry 13 of every row lies in 0.05 to 0.11, entries 4, 10, 12, 14, 16, 22 in 0.005 to 0.02, the others in -0.006 to 0.006.
All inputs are finite; a program needn't handle non-finite values.
Results may differ from a plain program's by a relative error of at most 0.00002.
Values sent between devices are 32-bit elements; how exact they have to be, the bound alone decides.
A program may use at most 128 MiB of HBM per device.

v0:
```python
import jax
import jax.numpy as jnp
from jax import lax
from jax.sharding import Mesh
from jax.sharding import PartitionSpec as P

LEVELS = 4
SWEEPS = 3
GX = ("gx_0", "gx_1")
GY = ("gy_0", "gy_1")
GX_GY = ("gx_0", "gx_1", "gy_0", "gy_1")


def extended(array, sides, width):
    for axis, dim in sides:
        peers, length = (lax.axis_size(axis), array.shape[dim])
        up = [(i, (i + 1) % peers) for i in range(peers - 1)]
        down = [(j, i) for i, j in up]
        last = lax.slice_in_dim(array, length - width, length, axis=dim)
        initial = lax.slice_in_dim(array, 0, width, axis=dim)
        before = lax.ppermute(last, axis, up)
        after = lax.ppermute(initial, axis, down)
        array = jnp.concatenate([before, array, after], axis=dim)
    return array


def sent_to_all(array, axis):
    peers = lax.axis_size(axis)
    return lax.all_to_all(
        jnp.broadcast_to(array[None], (peers, *array.shape)), axis, 0, 0, tiled=True
    )


def laid_out(blocks, dim):
    lengths = list(blocks.shape[1:])
    lengths[dim] *= blocks.shape[0]
    return jnp.moveaxis(blocks, 0, dim).reshape(lengths)


def collect(array, axis, dim):
    blocks = sent_to_all(array, axis)
    return laid_out(blocks, dim)


def one_axis_at_a_time(array, axes):
    for axis in axes:
        array = lax.psum(array, axis)
    return array


def shifted_sum(padded, weights, shape):
    total = jnp.zeros(shape, jnp.float32)
    for shift_first in range(3):
        for shift_second in range(3):
            for shift_third in range(3):
                window = padded[
                    shift_first : shift_first + shape[0],
                    shift_second : shift_second + shape[1],
                    shift_third : shift_third + shape[2],
                ]
                total = total + weights[9 * shift_first + 3 * shift_second + shift_third] * window
    return total


def weight_sums(cotangent, padded):
    shape = cotangent.shape
    sums = []
    for shift_first in range(3):
        for shift_second in range(3):
            for shift_third in range(3):
                window = padded[
                    shift_first : shift_first + shape[0],
                    shift_second : shift_second + shape[1],
                    shift_third : shift_third + shape[2],
                ]
                sums.append(jnp.sum(cotangent * window))
    return jnp.stack(sums)


def operate(padded, field, tally):
    beside = padded[2:, 1:-1, 1:-1] + padded[:-2, 1:-1, 1:-1]
    beside = beside + padded[1:-1, 2:, 1:-1] + padded[1:-1, :-2, 1:-1]
    beside = beside + padded[1:-1, 1:-1, 2:] + padded[1:-1, 1:-1, :-2]
    return (6.0 - tally) * field - beside


def restrict(field):
    shape = field.shape
    return field.reshape(shape[0] // 2, 2, shape[1] // 2, 2, shape[2]).mean(axis=(1, 3))


def prolong(field):
    return jnp.repeat(jnp.repeat(field, 2, axis=0), 2, axis=1)


def block_sums(field):
    shape = field.shape
    return field.reshape(shape[0] // 2, 2, shape[1] // 2, 2, shape[2]).sum(axis=(1, 3))


def face_tally(shape, start_first, start_second, total_first, total_second, face_mask):
    walls = face_mask.astype(jnp.float32)
    first = start_first + lax.broadcasted_iota(jnp.int32, shape, 0)
    second = start_second + lax.broadcasted_iota(jnp.int32, shape, 1)
    third = lax.broadcasted_iota(jnp.int32, shape, 2)
    tally = walls[0] * (first == 0).astype(jnp.float32) + walls[1] * (
        first == total_first - 1
    ).astype(jnp.float32)
    tally = (
        tally
        + walls[2] * (second == 0).astype(jnp.float32)
        + walls[3] * (second == total_second - 1).astype(jnp.float32)
    )
    tally = (
        tally
        + walls[4] * (third == 0).astype(jnp.float32)
        + walls[5] * (third == shape[2] - 1).astype(jnp.float32)
    )
    return tally


def level_tally(shape, face_mask):
    start_first = lax.axis_index(GX) * shape[0]
    start_second = lax.axis_index(GY) * shape[1]
    return face_tally(
        shape,
        start_first,
        start_second,
        shape[0] * lax.axis_size(GX),
        shape[1] * lax.axis_size(GY),
        face_mask,
    )


def loop_tally(shape, face_mask):
    start_first = lax.axis_index(GX) * shape[0] - 1
    start_second = lax.axis_index(GY) * shape[1] - 1
    wider = (shape[0] + 2, shape[1] + 2, shape[2])
    return face_tally(
        wider,
        start_first,
        start_second,
        shape[0] * lax.axis_size(GX),
        shape[1] * lax.axis_size(GY),
        face_mask,
    )


def loop_inside(shape):
    wider = (shape[0] + 2, shape[1] + 2, shape[2])
    first = lax.axis_index(GX) * shape[0] - 1 + lax.broadcasted_iota(jnp.int32, wider, 0)
    second = lax.axis_index(GY) * shape[1] - 1 + lax.broadcasted_iota(jnp.int32, wider, 1)
    inside = (
        (first >= 0)
        & (first < shape[0] * lax.axis_size(GX))
        & (second >= 0)
        & (second < shape[1] * lax.axis_size(GY))
    )
    return inside.astype(jnp.float32)


def coarse_tally(shape, face_mask):
    start_second = lax.axis_index(GY) * shape[1]
    return face_tally(shape, 0, start_second, shape[0], shape[1] * lax.axis_size(GY), face_mask)


def widen_level(field):
    rimmed = extended(field, ((GX, 0), (GY, 1)), 1)
    return jnp.pad(rimmed, ((0, 0), (0, 0), (1, 1)))


def widen_deep(field):
    rimmed = extended(field, ((GX, 0), (GY, 1)), 2)
    return jnp.pad(rimmed, ((0, 0), (0, 0), (1, 1)))


def smooth_then_apply(field, weights, tally):
    shape = field.shape
    deep = widen_deep(field)
    wider = (shape[0] + 2, shape[1] + 2, shape[2])
    smoothed_loop = shifted_sum(deep, weights, wider) * loop_inside(shape)
    smoothed = smoothed_loop[1:-1, 1:-1]
    applied = operate(jnp.pad(smoothed_loop, ((0, 0), (0, 0), (1, 1))), smoothed, tally)
    return (smoothed, applied, deep[1:-1, 1:-1])


def apply_then_smooth(middle, source_wide, weights, face_mask):
    shape = middle.shape
    deep = widen_deep(middle)
    source_loop = source_wide[:, :, 1:-1]
    applied_loop = operate(deep, deep[1:-1, 1:-1, 1:-1], loop_tally(shape, face_mask))
    after_loop = (source_loop - applied_loop) * loop_inside(shape)
    after_wide = jnp.pad(after_loop, ((0, 0), (0, 0), (1, 1)))
    after = after_loop[1:-1, 1:-1]
    smoothed = shifted_sum(after_wide, weights, shape)
    return (after, after_wide, smoothed)


def widen_coarse(field):
    rimmed = extended(field, ((GY, 1),), 1)
    return jnp.pad(rimmed, ((1, 1), (0, 0), (1, 1)))


def agglomerate(field):
    return collect(field, GX, 0)


def own_block(whole, shape):
    start_first = lax.axis_index(GX) * shape[0]
    block = lax.dynamic_slice_in_dim(whole, start_first, shape[0], 0)
    return block


def coarse_owner():
    return jnp.where(lax.axis_index(GX) == 0, 1.0, 0.0).astype(jnp.float32)


def on_device(rhs, target, stencils, face_mask):
    saved = []
    source = rhs
    for height in range(LEVELS):
        tally = level_tally(source.shape, face_mask)
        presmooth, applied, source_wide = smooth_then_apply(source, stencils[height], tally)
        remainder = source - applied
        saved.append((source, source_wide, presmooth, tally))
        source = restrict(remainder)
    coarse_shape = source.shape
    whole_source = agglomerate(source)
    whole_shape = whole_source.shape
    whole_tally = coarse_tally(whole_shape, face_mask)
    coarse_weights = stencils[2 * LEVELS]
    inputs = [widen_coarse(whole_source)]
    iterate = shifted_sum(inputs[0], coarse_weights, whole_shape)
    for sweep_index in range(SWEEPS - 1):
        remainder = whole_source - operate(widen_coarse(iterate), iterate, whole_tally)
        inputs.append(widen_coarse(remainder))
        iterate = iterate + shifted_sum(inputs[-1], coarse_weights, whole_shape)
    correction = own_block(iterate, coarse_shape)
    posts = [None] * LEVELS
    for height in reversed(range(LEVELS)):
        source, source_wide, presmooth, tally = saved[height]
        middle = presmooth + prolong(correction)
        after, after_wide, smoothed = apply_then_smooth(
            middle, source_wide, stencils[LEVELS + height], face_mask
        )
        correction = middle + smoothed
        posts[height] = (after, after_wide)
    error = correction - target
    grads = [None] * (2 * LEVELS + 1)
    upward = []
    cotangent = error
    for height in range(LEVELS):
        source, source_wide, presmooth, tally = saved[height]
        after, after_wide = posts[height]
        grads[LEVELS + height] = weight_sums(cotangent, after_wide)
        grad_after, applied, unused = smooth_then_apply(
            cotangent, stencils[LEVELS + height][::-1], tally
        )
        grad_middle = cotangent - applied
        upward.append((grad_after, grad_middle))
        cotangent = block_sums(grad_middle)
    grad_iterate = agglomerate(cotangent)
    flipped = coarse_weights[::-1]
    grad_source = jnp.zeros(whole_shape, jnp.float32)
    coarse_grad = jnp.zeros((27,), jnp.float32)
    for sweep_index in reversed(range(SWEEPS - 1)):
        coarse_grad = coarse_grad + weight_sums(grad_iterate, inputs[sweep_index + 1])
        grad_remainder = shifted_sum(widen_coarse(grad_iterate), flipped, whole_shape)
        grad_source = grad_source + grad_remainder
        grad_iterate = grad_iterate - operate(
            widen_coarse(grad_remainder), grad_remainder, whole_tally
        )
    coarse_grad = coarse_grad + weight_sums(grad_iterate, inputs[0])
    grad_source = grad_source + shifted_sum(widen_coarse(grad_iterate), flipped, whole_shape)
    grads[2 * LEVELS] = coarse_grad * coarse_owner()
    grad_down = own_block(grad_source, coarse_shape)
    for height in reversed(range(LEVELS)):
        source, source_wide, presmooth, tally = saved[height]
        grad_after, grad_middle = upward[height]
        grad_remainder = 0.25 * prolong(grad_down)
        grad_level = grad_after + grad_remainder
        grad_pre = grad_middle - operate(widen_level(grad_remainder), grad_remainder, tally)
        grads[height] = weight_sums(grad_pre, source_wide)
        grad_level = grad_level + shifted_sum(
            widen_level(grad_pre), stencils[height][::-1], source.shape
        )
        grad_down = grad_level
    totals = one_axis_at_a_time(jnp.stack(grads), GX_GY)
    cells_total = rhs.shape[0] * lax.axis_size(GX) * rhs.shape[1] * lax.axis_size(GY) * rhs.shape[2]
    return (correction, grad_down, totals / cells_total)


def solution(mesh):
    torus = Mesh(mesh.devices.reshape(4, 8, 8, 2), ("gx_0", "gx_1", "gy_0", "gy_1"))
    return jax.shard_map(
        on_device,
        mesh=torus,
        in_specs=(P(GX, GY, None), P(GX, GY, None), P(), P()),
        out_specs=(P(GX, GY, None), P(GX, GY, None), P()),
        check_vma=False,
    )
```

profile of v0, /device:TPU:1, one launch (start us, length us, event | category | flops | bytes accessed | tf_op | source)
XLA Modules:
  0.0 1164.6 jit_solution(2048301961063207728)
XLA Ops:
  43.3 18.5 %fusion.109 = f32[18,34,128]{2,1,0:T(8,128)S(1)} fusion(f32[20,36,128]{2,1,0:T(8,128)S(1)} %pad_maximum_fusion, f32[20,2,128]{2,1,0:T(2,128)S(1)} %collective-permute-done.3, f32[20,32,128]{2,1,0:T(8,128)S(1)} %constant_dynamic-update-slice_fusion, f32[20,2,128]{2,1,0:T(2,128)S(1)} %collective-permute-done.2, f32[]{:T(128)} %bitcast.26, f32[]{:T(128)} %bitcast.25, ...), kind=kLoop, calls=%fused_computation.426 | loop fusion | flops 4856832 | bytes 2199148 | tf_op jit(solution)/shard_map/mul | solution.py:181
  78.4 18.2 %fusion.302 = f32[10,18,128]{2,1,0:T(8,128)S(1)} fusion(f32[12,20,128]{2,1,0:T(8,128)S(1)} %pad_maximum_fusion.25, f32[12,18,128]{2,1,0:T(8,128)S(1)} %get-tuple-element.380, f32[12,18,128]{2,1,0:T(8,128)S(1)} %get-tuple-element.379, f32[]{:T(128)} %bitcast.60, f32[]{:T(128)} %bitcast.59, f32[]{:T(128)} %bitcast.58, f32[]{:T(128)} %bitcast.57, f32[]{:T(128)} %bitcast.56, ...), kind=kLoop, calls=%fused_computation.781 | loop fusion | flops 1290240 | bytes 1345690 | tf_op jit(solution)/shard_map/mul | solution.py:181
  115.0 17.7 %fusion.489 = f32[6,10,128]{2,1,0:T(8,128)S(1)} fusion(f32[8,12,128]{2,1,0:T(8,128)S(1)} %pad_maximum_fusion.49, f32[8,10,128]{2,1,0:T(8,128)S(1)} %get-tuple-element.426, f32[8,10,128]{2,1,0:T(8,128)S(1)} %get-tuple-element.425, f32[]{:T(128)} %bitcast.88, f32[]{:T(128)} %bitcast.87, f32[]{:T(128)} %bitcast.86, f32[]{:T(128)} %bitcast.85, f32[]{:T(128)} %bitcast.84, ...), kind=kLoop, calls=%fused_computation.1098 | loop fusion | flops 430080 | bytes 539264 | tf_op jit(solution)/shard_map/mul | solution.py:181
  148.8 17.6 %fusion.690 = f32[4,6,128]{2,1,0:T(8,128)S(1)} fusion(f32[6,8,128]{2,1,0:T(8,128)S(1)} %pad_maximum_fusion.81, f32[6,6,128]{2,1,0:T(8,128)S(1)} %get-tuple-element.450, f32[6,6,128]{2,1,0:T(8,128)S(1)} %get-tuple-element.449, f32[]{:T(128)} %bitcast.116, f32[]{:T(128)} %bitcast.115, f32[]{:T(128)} %bitcast.114, f32[]{:T(128)} %bitcast.113, f32[]{:T(128)} %bitcast.112, ...), kind=kLoop, calls=%fused_computation.1541 | loop fusion | flops 172032 | bytes 184952 | tf_op jit(solution)/shard_map/mul | solution.py:181
  199.6 17.4 %multiply_add_fusion.1 = f32[32,2,128]{2,1,0:T(2,128)S(1)} fusion(f32[32,2,128]{2,1,0:T(2,128)S(1)} %bitcast.640, f32[34,4,130]{2,1,0:T(4,128)S(1)} %select_maximum_fusion.34, f32[]{:T(128)} %bitcast.145, f32[]{:T(128)} %bitcast.144, f32[]{:T(128)} %bitcast.143, f32[]{:T(128)} %bitcast.142, f32[]{:T(128)} %bitcast.141, f32[]{:T(128)} %bitcast.140, ...), kind=kLoop, calls=%fused_computation.1426 | loop fusion | flops 450560 | bytes 884844 | tf_op jit(solution)/shard_map/add | solution.py:61
  236.3 17.4 %add_add_fusion.2 = f32[32,2,128]{2,1,0:T(2,128)S(1)} fusion(f32[32,2,128]{2,1,0:T(2,128)S(1)} %multiply_add_fusion.1, f32[32,2,128]{2,1,0:T(2,128)S(1)} %fusion.588, f32[34,4,130]{2,1,0:T(4,128)S(1)} %select_maximum_fusion.30, f32[]{:T(128)} %bitcast.145, f32[]{:T(128)} %bitcast.144, f32[]{:T(128)} %bitcast.143, f32[]{:T(128)} %bitcast.142, f32[]{:T(128)} %bitcast.141, ...), kind=kLoop, calls=%fused_computation.1424 | loop fusion | flops 458752 | bytes 917612 | tf_op jit(solution)/shard_map/add | solution.py:237
  374.3 17.2 %add_add_fusion.1 = f32[8,16,128]{2,1,0:T(8,128)S(1)} fusion(f32[8,16,128]{2,1,0:T(8,128)S(1)} %slice_add_fusion.19, f32[10,18,128]{2,1,0:T(8,128)S(1)} %fusion.216, f32[]{:T(128)} %bitcast.232, f32[]{:T(128)} %bitcast.231, f32[]{:T(128)} %bitcast.230, f32[]{:T(128)} %bitcast.229, f32[]{:T(128)} %bitcast.228, f32[]{:T(128)} %bitcast.227, f32[]{:T(128)} %bitcast.226, ...), kind=kLoop, calls=%fused_computation.1003 | loop fusion | flops 884736 | bytes 843884 | tf_op jit(solution)/shard_map/add | solution.py:246
  410.7 20.5 %multiply_reduce_fusion = (f32[]{:T(128)}, f32[]{:T(128)}, f32[]{:T(128)}, f32[]{:T(128)}, f32[]{:T(128)}, /*index=5*/f32[]{:T(128)}, f32[]{:T(128)}, f32[]{:T(1...) fusion(f32[18,34,128]{2,1,0:T(8,128)S(1)} %fusion.43, ...), kind=kLoop, calls=%fused_computation.577 | loop fusion | flops 5963758 | bytes 3776692 | tf_op jit(solution)/shard_map/reduce_sum | solution.py:76
  449.2 18.6 %fusion.86 = f32[18,34,128]{2,1,0:T(8,128)S(1)} fusion(f32[20,36,128]{2,1,0:T(8,128)S(1)} %pad_maximum_fusion.2, f32[20,34,128]{2,1,0:T(8,128)S(1)} %get-tuple-element.340, f32[20,34,128]{2,1,0:T(8,128)S(1)} %get-tuple-element.339, f32[]{:T(128)} %bitcast.235, f32[]{:T(128)} %bitcast.236, f32[]{:T(128)} %bitcast.237, f32[]{:T(128)} %bitcast.238, ...), kind=kLoop, calls=%fused_computation.379 | loop fusion | flops 4386816 | bytes 4042348 | tf_op jit(solution)/shard_map/mul | solution.py:181
  485.6 18.1 %fusion.258 = f32[10,18,128]{2,1,0:T(8,128)S(1)} fusion(f32[12,20,128]{2,1,0:T(8,128)S(1)} %pad_maximum_fusion.28, f32[12,18,128]{2,1,0:T(8,128)S(1)} %get-tuple-element.374, f32[12,18,128]{2,1,0:T(8,128)S(1)} %get-tuple-element.373, f32[]{:T(128)} %bitcast.206, f32[]{:T(128)} %bitcast.207, f32[]{:T(128)} %bitcast.208, f32[]{:T(128)} %bitcast.209, ...), kind=kLoop, calls=%fused_computation.737 | loop fusion | flops 1290240 | bytes 1345690 | tf_op jit(solution)/shard_map/mul | solution.py:181
  526.2 17.6 %fusion.445 = f32[6,10,128]{2,1,0:T(8,128)S(1)} fusion(f32[8,12,128]{2,1,0:T(8,128)S(1)} %pad_maximum_fusion.52, f32[8,10,128]{2,1,0:T(8,128)S(1)} %get-tuple-element.410, f32[8,10,128]{2,1,0:T(8,128)S(1)} %get-tuple-element.409, f32[]{:T(128)} %bitcast.177, f32[]{:T(128)} %bitcast.178, f32[]{:T(128)} %bitcast.179, f32[]{:T(128)} %bitcast.180, ...), kind=kLoop, calls=%fused_computation.1054 | loop fusion | flops 430080 | bytes 539264 | tf_op jit(solution)/shard_map/mul | solution.py:181
  563.1 17.5 %fusion.646 = f32[4,6,128]{2,1,0:T(8,128)S(1)} fusion(f32[6,8,128]{2,1,0:T(8,128)S(1)} %pad_maximum_fusion.84, f32[6,6,128]{2,1,0:T(8,128)S(1)} %get-tuple-element.444, f32[6,6,128]{2,1,0:T(8,128)S(1)} %get-tuple-element.443, f32[]{:T(128)} %bitcast.148, f32[]{:T(128)} %bitcast.149, f32[]{:T(128)} %bitcast.150, f32[]{:T(128)} %bitcast.151, f32[]{:T(128)} %bitcast.152, ...), kind=kLoop, calls=%fused_computation.1497 | loop fusion | flops 172032 | bytes 184952 | tf_op jit(solution)/shard_map/mul | solution.py:181
  583.8 21.6 %all_to_all.10 = f32[32,1,2,128]{3,2,1,0:T(2,128)S(1)} all-to-all(f32[32,1,2,128]{3,2,1,0:T(2,128)S(1)} %broadcast_in_dim.84), channel_id=1, replica_groups=mesh['gx_0'=4,'gx_1'=8,'gy_0'=8,'gy_1'=2] {'gx_0','gx_1'}, dimensions={0} | all-to-all | bytes 65536 | tf_op jit(solution)/shard_map/all_to_all | solution.py:29
  615.5 17.4 %fusion.555 = f32[32,2,128]{2,1,0:T(2,128)S(1)} fusion(f32[34,4,130]{2,1,0:T(4,128)S(1)} %select_maximum_fusion.24, f32[32,1,128]{2,1,0:T(1,128)S(1)} %collective-permute-done.59, f32[32,2,128]{2,1,0:T(2,128)S(1)} %bitcast.648, f32[32,1,128]{2,1,0:T(1,128)S(1)} %collective-permute-done.58, f32[]{:T(128)} %bitcast.145, f32[]{:T(128)} %bitcast.144, ...), kind=kLoop, calls=%fused_computation.1265 | loop fusion | flops 450560 | bytes 884844 | tf_op jit(solution)/shard_map/add | solution.py:61
  653.3 17.2 %stack.1095 = f32[27]{0:T(128)} concatenate(f32[1]{0:T(128)} %bitcast.400, f32[1]{0:T(128)} %bitcast.401, f32[1]{0:T(128)} %bitcast.402, f32[1]{0:T(128)} %bitcast.403, f32[1]{0:T(128)} %bitcast.404, f32[1]{0:T(128)} %bitcast.405, f32[1]{0:T(128)} %bitcast.406, f32[1]{0:T(128)} %bitcast.407, f32[1]{0:T(128)} %bitcast.408, f32[1]{0:T(128)} %bitcast.409, f32[1]{0:T(128)} %bitcast.410, ...), dimensions={0} | concatenate | bytes 216 | tf_op jit(solution)/shard_map/stack | solution.py:77
  671.5 18.1 %fusion.523 = f32[32,2,128]{2,1,0:T(2,128)S(1)} fusion(f32[34,4,130]{2,1,0:T(4,128)S(1)} %select_maximum_fusion.20, f32[32,1,128]{2,1,0:T(1,128)} %collective-permute-done.63, f32[32,2,128]{2,1,0:T(2,128)S(1)} %copy-done.12, f32[32,1,128]{2,1,0:T(1,128)} %collective-permute-done.62, f32[]{:T(128)} %bitcast.145, f32[]{:T(128)} %bitcast.144, f32[]{:T(128)} %bitcast.143, ...), kind=kLoop, calls=%fused_computation.1202 | loop fusion | flops 450560 | bytes 884844 | tf_op jit(solution)/shard_map/add | solution.py:61
  733.0 17.4 %stack.1124 = f32[27]{0:T(128)} concatenate(f32[1]{0:T(128)} %bitcast.428, f32[1]{0:T(128)} %bitcast.429, f32[1]{0:T(128)} %bitcast.430, f32[1]{0:T(128)} %bitcast.431, f32[1]{0:T(128)} %bitcast.432, f32[1]{0:T(128)} %bitcast.433, f32[1]{0:T(128)} %bitcast.434, f32[1]{0:T(128)} %bitcast.435, f32[1]{0:T(128)} %bitcast.436, f32[1]{0:T(128)} %bitcast.437, f32[1]{0:T(128)} %bitcast.438, ...), dimensions={0} | concatenate | bytes 216 | tf_op jit(solution)/shard_map/stack | solution.py:77
  773.7 17.5 %stack.1153 = f32[27]{0:T(128)} concatenate(f32[1]{0:T(128)} %bitcast.456, f32[1]{0:T(128)} %bitcast.457, f32[1]{0:T(128)} %bitcast.458, f32[1]{0:T(128)} %bitcast.459, f32[1]{0:T(128)} %bitcast.460, f32[1]{0:T(128)} %bitcast.461, f32[1]{0:T(128)} %bitcast.462, f32[1]{0:T(128)} %bitcast.463, f32[1]{0:T(128)} %bitcast.464, f32[1]{0:T(128)} %bitcast.465, f32[1]{0:T(128)} %bitcast.466, ...), dimensions={0} | concatenate | bytes 216 | tf_op jit(solution)/shard_map/stack | solution.py:77
  791.4 17.6 %fusion.816 = f32[2,4,128]{2,1,0:T(4,128)S(1)} fusion(f32[4,6,130]{2,1,0:T(8,128)S(1)} %select_maximum_fusion.44, f32[4,1,128]{2,1,0:T(1,128)S(1)} %collective-permute-done.75, f32[1,4,128]{2,1,0:T(4,128)S(1)} %collective-permute-done.73, f32[2,4,128]{2,1,0:T(4,128)S(1)} %get-tuple-element.333, f32[1,4,128]{2,1,0:T(4,128)S(1)} %collective-permute-done.72, ...), kind=kLoop, calls=%fused_computation.1824 | loop fusion | flops 77824 | bytes 96364 | tf_op jit(solution)/shard_map/mul | solution.py:280
  823.5 17.8 %stack.1182 = f32[27]{0:T(128)} concatenate(f32[1]{0:T(128)} %bitcast.484, f32[1]{0:T(128)} %bitcast.485, f32[1]{0:T(128)} %bitcast.486, f32[1]{0:T(128)} %bitcast.487, f32[1]{0:T(128)} %bitcast.488, f32[1]{0:T(128)} %bitcast.489, f32[1]{0:T(128)} %bitcast.490, f32[1]{0:T(128)} %bitcast.491, f32[1]{0:T(128)} %bitcast.492, f32[1]{0:T(128)} %bitcast.493, f32[1]{0:T(128)} %bitcast.494, ...), dimensions={0} | concatenate | bytes 216 | tf_op jit(solution)/shard_map/stack | solution.py:77
  876.4 17.6 %fusion.723 = f32[4,8,128]{2,1,0:T(8,128)S(1)} fusion(f32[6,10,130]{2,1,0:T(8,128)S(1)} %select_maximum_fusion.36, f32[6,9,128]{2,1,0:T(8,128)S(1)} %get-tuple-element.430, f32[1,8,128]{2,1,0:T(8,128)S(1)} %collective-permute-done.81, f32[4,8,128]{2,1,0:T(8,128)S(1)} %get-tuple-element.334, f32[6,9,128]{2,1,0:T(8,128)S(1)} %get-tuple-element.429, ...), kind=kLoop, calls=%fused_computation.1583 | loop fusion | flops 237568 | bytes 467052 | tf_op jit(solution)/shard_map/mul | solution.py:280
  1069.3 21.0 %psum.28 = f32[9,27]{1,0:T(8,128)S(1)} all-reduce(f32[9,27]{1,0:T(8,128)S(1)} %stack.1268), channel_id=1, replica_groups=mesh['gx_0'=4,'gx_1'=8,'gy_0'=8,'gy_1'=2] {'gx_0'}, use_global_device_ids=true, to_apply=%region_307.308 | all-reduce | flops 243 | bytes 1944 | tf_op jit(solution)/shard_map/psum | solution.py:47
  1101.2 23.2 %psum.30 = f32[9,27]{1,0:T(8,128)S(1)} all-reduce(f32[9,27]{1,0:T(8,128)S(1)} %psum.29), channel_id=1, replica_groups=mesh['gx_0'=4,'gx_1'=8,'gy_0'=8,'gy_1'=2] {'gy_0'}, use_global_device_ids=true, to_apply=%region_309.310 | all-reduce | flops 243 | bytes 1944 | tf_op jit(solution)/shard_map/psum | solution.py:47
  1145.7 18.4 %fusion.175 = f32[16,32,128]{2,1,0:T(8,128)} fusion(f32[18,34,130]{2,1,0:T(8,128)S(1)} %select_maximum_fusion, f32[18,33,128]{2,1,0:T(8,128)S(1)} %get-tuple-element.348, f32[1,32,128]{2,1,0:T(8,128)S(1)} %collective-permute-done.97, f32[16,32,128]{2,1,0:T(8,128)S(1)} %get-tuple-element.336, f32[18,33,128]{2,1,0:T(8,128)S(1)} %get-tuple-element.347, ...), kind=kLoop, calls=%fused_computation.503 | loop fusion | flops 3735552 | bytes 7372908 | tf_op jit(solution)/shard_map/add | solution.py:284
  (700 shorter events, 718.5 us)
Async XLA Ops:
  1.5 30.2 %collective-permute-start.1 = (f32[2,32,128]{2,1,0:T(8,128)S(1)}, f32[2,32,128]{2,1,0:T(8,128)S(1)}, u32[]{:S(2)}, u32[]{:S(2)}) collective-permute-start(f32[2,32,128]{2,1,0:T(8,128)S(1)} %get-tuple-element.359), channel_id=1, source_target_pairs={{16,0},{32,16},{48,32},{64,48},{80,64},{96,80},{112,96},{128,112},... | collective-permute-start | bytes 98312 | tf_op jit(solution)/shard_map/ppermute | solution.py:22
  2.8 28.2 %collective-permute-start = (f32[2,32,128]{2,1,0:T(8,128)S(1)}, f32[2,32,128]{2,1,0:T(8,128)S(1)}, u32[]{:S(2)}, u32[]{:S(2)}) collective-permute-start(f32[2,32,128]{2,1,0:T(8,128)S(1)} %get-tuple-element.360), channel_id=1, source_target_pairs={{0,16},{16,32},{32,48},{48,64},{64,80},{80,96},{96,112},{112,128},... | collective-permute-start | bytes 98312 | tf_op jit(solution)/shard_map/ppermute | solution.py:21
  167.3 23.0 %all-to-all-start = ((f32[32,1,2,128]{3,2,1,0:T(2,128)}), f32[32,1,2,128]{3,2,1,0:T(2,128)S(1)}, u32[]{:S(2)}, u32[]{:S(2)}) async-start(f32[32,1,2,128]{3,2,1,0:T(2,128)} %broadcast_in_dim.74), calls=%async_computation | async-start | bytes 65536 | tf_op jit(solution)/shard_map/all_to_all | solution.py:29
  647.2 23.3 %collective-permute-start.62 = (f32[32,1,128]{2,1,0:T(1,128)}, f32[32,1,128]{2,1,0:T(1,128)}, u32[]{:S(2)}, u32[]{:S(2)}) collective-permute-start(f32[32,1,128]{2,1,0:T(1,128)} %get-tuple-element.403), channel_id=1, source_target_pairs={{0,1},{1,2},{2,3},{3,4},{4,5},{5,6},{6,7},{7,8},{8,9},{9,10},{10,1... | collective-permute-start | bytes 49160 | tf_op jit(solution)/shard_map/ppermute | solution.py:21
  649.6 21.0 %collective-permute-start.63 = (f32[32,1,128]{2,1,0:T(1,128)}, f32[32,1,128]{2,1,0:T(1,128)}, u32[]{:S(2)}, u32[]{:S(2)}) collective-permute-start(f32[32,1,128]{2,1,0:T(1,128)} %get-tuple-element.404), channel_id=1, source_target_pairs={{1,0},{2,1},{3,2},{4,3},{5,4},{6,5},{7,6},{8,7},{9,8},{10,9},{11,1... | collective-permute-start | bytes 49160 | tf_op jit(solution)/shard_map/ppermute | solution.py:22
  729.4 21.1 %collective-permute-start.69 = (f32[1,4,128]{2,1,0:T(4,128)S(1)}, f32[1,4,128]{2,1,0:T(4,128)S(1)}, u32[]{:S(2)}, u32[]{:S(2)}) collective-permute-start(f32[1,4,128]{2,1,0:T(4,128)S(1)} %bitcast.670), channel_id=1, source_target_pairs={{0,16},{16,32},{32,48},{48,64},{64,80},{80,96},{96,112},{112,128},... | collective-permute-start | bytes 6152 | tf_op jit(solution)/shard_map/ppermute | solution.py:21
  768.4 22.8 %collective-permute-start.74 = (f32[4,1,128]{2,1,0:T(1,128)S(1)}, f32[4,1,128]{2,1,0:T(1,128)S(1)}, u32[]{:S(2)}, u32[]{:S(2)}) collective-permute-start(f32[4,1,128]{2,1,0:T(1,128)S(1)} %get-tuple-element.455), channel_id=1, source_target_pairs={{0,1},{1,2},{2,3},{3,4},{4,5},{5,6},{6,7},{7,8},{8,9},{9,10},{10,1... | collective-permute-start | bytes 6152 | tf_op jit(solution)/shard_map/ppermute | solution.py:21
  771.8 19.4 %collective-permute-start.75 = (f32[4,1,128]{2,1,0:T(1,128)S(1)}, f32[4,1,128]{2,1,0:T(1,128)S(1)}, u32[]{:S(2)}, u32[]{:S(2)}) collective-permute-start(f32[4,1,128]{2,1,0:T(1,128)S(1)} %get-tuple-element.456), channel_id=1, source_target_pairs={{1,0},{2,1},{3,2},{4,3},{5,4},{6,5},{7,6},{8,7},{9,8},{10,9},{11,1... | collective-permute-start | bytes 6152 | tf_op jit(solution)/shard_map/ppermute | solution.py:22
  815.2 26.2 %collective-permute-start.79 = (f32[6,1,128]{2,1,0:T(1,128)S(1)}, f32[6,1,128]{2,1,0:T(1,128)S(1)}, u32[]{:S(2)}, u32[]{:S(2)}) collective-permute-start(f32[6,1,128]{2,1,0:T(1,128)S(1)} %get-tuple-element.433), channel_id=1, source_target_pairs={{0,1},{1,2},{2,3},{3,4},{4,5},{5,6},{6,7},{7,8},{8,9},{9,10},{10,1... | collective-permute-start | bytes 9224 | tf_op jit(solution)/shard_map/ppermute | solution.py:21
  820.8 20.5 %collective-permute-start.78 = (f32[6,1,128]{2,1,0:T(1,128)S(1)}, f32[6,1,128]{2,1,0:T(1,128)S(1)}, u32[]{:S(2)}, u32[]{:S(2)}) collective-permute-start(f32[6,1,128]{2,1,0:T(1,128)S(1)} %get-tuple-element.434), channel_id=1, source_target_pairs={{1,0},{2,1},{3,2},{4,3},{5,4},{6,5},{7,6},{8,7},{9,8},{10,9},{11,1... | collective-permute-start | bytes 9224 | tf_op jit(solution)/shard_map/ppermute | solution.py:22
  851.2 25.0 %collective-permute-start.82 = (f32[6,1,128]{2,1,0:T(1,128)S(1)}, f32[6,1,128]{2,1,0:T(1,128)S(1)}, u32[]{:S(2)}, u32[]{:S(2)}) collective-permute-start(f32[6,1,128]{2,1,0:T(1,128)S(1)} %get-tuple-element.431), channel_id=1, source_target_pairs={{0,1},{1,2},{2,3},{3,4},{4,5},{5,6},{6,7},{7,8},{8,9},{9,10},{10,1... | collective-permute-start | bytes 9224 | tf_op jit(solution)/shard_map/ppermute | solution.py:21
  856.3 20.0 %collective-permute-start.83 = (f32[6,1,128]{2,1,0:T(1,128)S(1)}, f32[6,1,128]{2,1,0:T(1,128)S(1)}, u32[]{:S(2)}, u32[]{:S(2)}) collective-permute-start(f32[6,1,128]{2,1,0:T(1,128)S(1)} %get-tuple-element.432), channel_id=1, source_target_pairs={{1,0},{2,1},{3,2},{4,3},{5,4},{6,5},{7,6},{8,7},{9,8},{10,9},{11,1... | collective-permute-start | bytes 9224 | tf_op jit(solution)/shard_map/ppermute | solution.py:22
  894.1 22.7 %collective-permute-start.84 = (f32[1,16,128]{2,1,0:T(8,128)S(1)}, f32[1,16,128]{2,1,0:T(8,128)S(1)}, u32[]{:S(2)}, u32[]{:S(2)}) collective-permute-start(f32[1,16,128]{2,1,0:T(8,128)S(1)} %bitcast.680), channel_id=1, source_target_pairs={{16,0},{32,16},{48,32},{64,48},{80,64},{96,80},{112,96},{128,112},... | collective-permute-start | bytes 24584 | tf_op jit(solution)/shard_map/ppermute | solution.py:22
  895.4 21.4 %collective-permute-start.85 = (f32[1,16,128]{2,1,0:T(8,128)S(1)}, f32[1,16,128]{2,1,0:T(8,128)S(1)}, u32[]{:S(2)}, u32[]{:S(2)}) collective-permute-start(f32[1,16,128]{2,1,0:T(8,128)S(1)} %bitcast.681), channel_id=1, source_target_pairs={{0,16},{16,32},{32,48},{48,64},{64,80},{80,96},{96,112},{112,128},... | collective-permute-start | bytes 24584 | tf_op jit(solution)/shard_map/ppermute | solution.py:21
  916.8 23.6 %collective-permute-start.87 = (f32[10,1,128]{2,1,0:T(1,128)S(1)}, f32[10,1,128]{2,1,0:T(1,128)S(1)}, u32[]{:S(2)}, u32[]{:S(2)}) collective-permute-start(f32[10,1,128]{2,1,0:T(1,128)S(1)} %get-tuple-element.387), channel_id=1, source_target_pairs={{0,1},{1,2},{2,3},{3,4},{4,5},{5,6},{6,7},{7,8},{8,9},{9,10},{10,1... | collective-permute-start | bytes 15368 | tf_op jit(solution)/shard_map/ppermute | solution.py:21
  921.0 19.4 %collective-permute-start.86 = (f32[10,1,128]{2,1,0:T(1,128)S(1)}, f32[10,1,128]{2,1,0:T(1,128)S(1)}, u32[]{:S(2)}, u32[]{:S(2)}) collective-permute-start(f32[10,1,128]{2,1,0:T(1,128)S(1)} %get-tuple-element.388), channel_id=1, source_target_pairs={{1,0},{2,1},{3,2},{4,3},{5,4},{6,5},{7,6},{8,7},{9,8},{10,9},{11,1... | collective-permute-start | bytes 15368 | tf_op jit(solution)/shard_map/ppermute | solution.py:22
  952.2 24.3 %collective-permute-start.90 = (f32[10,1,128]{2,1,0:T(1,128)S(1)}, f32[10,1,128]{2,1,0:T(1,128)S(1)}, u32[]{:S(2)}, u32[]{:S(2)}) collective-permute-start(f32[10,1,128]{2,1,0:T(1,128)S(1)} %get-tuple-element.385), channel_id=1, source_target_pairs={{0,1},{1,2},{2,3},{3,4},{4,5},{5,6},{6,7},{7,8},{8,9},{9,10},{10,1... | collective-permute-start | bytes 15368 | tf_op jit(solution)/shard_map/ppermute | solution.py:21
  957.0 19.5 %collective-permute-start.91 = (f32[10,1,128]{2,1,0:T(1,128)S(1)}, f32[10,1,128]{2,1,0:T(1,128)S(1)}, u32[]{:S(2)}, u32[]{:S(2)}) collective-permute-start(f32[10,1,128]{2,1,0:T(1,128)S(1)} %get-tuple-element.386), channel_id=1, source_target_pairs={{1,0},{2,1},{3,2},{4,3},{5,4},{6,5},{7,6},{8,7},{9,8},{10,9},{11,1... | collective-permute-start | bytes 15368 | tf_op jit(solution)/shard_map/ppermute | solution.py:22
  993.9 24.6 %collective-permute-start.92 = (f32[1,32,128]{2,1,0:T(8,128)S(1)}, f32[1,32,128]{2,1,0:T(8,128)S(1)}, u32[]{:S(2)}, u32[]{:S(2)}) collective-permute-start(f32[1,32,128]{2,1,0:T(8,128)S(1)} %bitcast.676), channel_id=1, source_target_pairs={{16,0},{32,16},{48,32},{64,48},{80,64},{96,80},{112,96},{128,112},... | collective-permute-start | bytes 49160 | tf_op jit(solution)/shard_map/ppermute | solution.py:22
  995.2 23.3 %collective-permute-start.93 = (f32[1,32,128]{2,1,0:T(8,128)S(1)}, f32[1,32,128]{2,1,0:T(8,128)S(1)}, u32[]{:S(2)}, u32[]{:S(2)}) collective-permute-start(f32[1,32,128]{2,1,0:T(8,128)S(1)} %bitcast.677), channel_id=1, source_target_pairs={{0,16},{16,32},{32,48},{48,64},{64,80},{80,96},{96,112},{112,128},... | collective-permute-start | bytes 49160 | tf_op jit(solution)/shard_map/ppermute | solution.py:21
  1018.7 24.0 %collective-permute-start.95 = (f32[18,1,128]{2,1,0:T(1,128)S(1)}, f32[18,1,128]{2,1,0:T(1,128)S(1)}, u32[]{:S(2)}, u32[]{:S(2)}) collective-permute-start(f32[18,1,128]{2,1,0:T(1,128)S(1)} %get-tuple-element.351), channel_id=1, source_target_pairs={{0,1},{1,2},{2,3},{3,4},{4,5},{5,6},{6,7},{7,8},{8,9},{9,10},{10,1... | collective-permute-start | bytes 27656 | tf_op jit(solution)/shard_map/ppermute | solution.py:21
  1022.6 20.1 %collective-permute-start.94 = (f32[18,1,128]{2,1,0:T(1,128)S(1)}, f32[18,1,128]{2,1,0:T(1,128)S(1)}, u32[]{:S(2)}, u32[]{:S(2)}) collective-permute-start(f32[18,1,128]{2,1,0:T(1,128)S(1)} %get-tuple-element.352), channel_id=1, source_target_pairs={{1,0},{2,1},{3,2},{4,3},{5,4},{6,5},{7,6},{8,7},{9,8},{10,9},{11,1... | collective-permute-start | bytes 27656 | tf_op jit(solution)/shard_map/ppermute | solution.py:22
  1044.8 91.7 %collective-permute-start.96 = (f32[1,32,128]{2,1,0:T(8,128)S(1)}, f32[1,32,128]{2,1,0:T(8,128)S(1)}, u32[]{:S(2)}, u32[]{:S(2)}) collective-permute-start(f32[1,32,128]{2,1,0:T(8,128)S(1)} %get-tuple-element.353), channel_id=1, source_target_pairs={{0,16},{16,32},{32,48},{48,64},{64,80},{80,96},{96,112},{112,128},... | collective-permute-start | bytes 49160 | tf_op jit(solution)/shard_map/ppermute | solution.py:21
  1048.4 88.0 %collective-permute-start.97 = (f32[1,32,128]{2,1,0:T(8,128)S(1)}, f32[1,32,128]{2,1,0:T(8,128)S(1)}, u32[]{:S(2)}, u32[]{:S(2)}) collective-permute-start(f32[1,32,128]{2,1,0:T(8,128)S(1)} %get-tuple-element.354), channel_id=1, source_target_pairs={{16,0},{32,16},{48,32},{64,48},{80,64},{96,80},{112,96},{128,112},... | collective-permute-start | bytes 49160 | tf_op jit(solution)/shard_map/ppermute | solution.py:22
  (211 other events, 3211.4 us)
where the time goes:
time: 1190 us; the launch traced here: 1160 us
  other arithmetic  459 us (39%)
  starting transfers between devices  292 us (25%)
  local copies, waits for them, and re-layouts  219 us (18%)
  waiting for transfers between devices  101 us (8%)
  blocking collectives  88.7 us (7%)
    ppermute x50, starting transfers between devices, extended(): before = lax.ppermute(last, axis, up)  189 us
    another operation x11, local copies, waits for them, and re-layouts, weight_sums(): return jnp.stack(sums)  187 us
    mul x8, other arithmetic, smooth_then_apply(): smoothed_loop = shifted_sum(deep, weights, wider) * loop_inside(shape)  144 us
    ppermute x50, waiting for transfers between devices, extended(): after = lax.ppermute(initial, axis, down)  92.4 us
    ppermute x50, starting transfers between devices, extended(): after = lax.ppermute(initial, axis, down)  89 us
    add x5, other arithmetic, shifted_sum(): total + weights[9 * shift_first + 3 * shift_second + shift_third] * window  81 us
    psum x4, blocking collectives, one_axis_at_a_time(): array = lax.psum(array, axis)  67.1 us
    mul x4, other arithmetic, on_device(): grad_remainder = 0.25 * prolong(grad_down)  55.4 us
  transfers between devices with their start and end apart: 101, of which 35 were waited for; matrix products, arithmetic and copies ran while one was open for 21% of the time, Pallas kernels for 0%

commit v1 on v0

v1 whole, which is shorter than its diff:
```python
import functools

import jax
import jax.numpy as jnp
from jax import lax
from jax.experimental import pallas as pl
from jax.experimental.pallas import tpu as pltpu
from jax.sharding import PartitionSpec as P

MESH = pl.DeviceIdType.MESH
LEVELS = 4
NZ = 128
CHUNK = 64
RIM = (3, 4, 5, 5, 7)
KNOWN = ((0, 0), (0, 0), (1, 0), (1, 1), (1, 1))
SCALES = tuple(4.0**level for level in range(LEVELS + 1))


def pieces(level, block, axis):
    rim = RIM[level]
    if level <= 1:
        return [(-1, block - rim, rim, False), (0, 0, block, False), (1, 0, rim, False)]
    if level == 2:
        if axis == 0:
            return [(-1, -1, 4, False), (0, -1, 6, False), (1, 1, 4, False)]
        return [(-1, 3, 5, False), (0, 0, 8, False), (1, 0, 5, False)]
    if level == 3:
        if axis == 0:
            return [(-2, -1, 4, True), (0, -1, 4, False), (2, -1, 4, True)]
        return [(-1, -1, 4, False), (0, -1, 6, False), (1, 1, 4, False)]
    if axis == 0:
        return [(d, -1, 3, d != 0) for d in (-6, -3, 0, 3, 6)]
    return [(-3, -1, 2, False), (-2, -1, 4, True), (0, -1, 4, False), (2, -1, 4, True), (3, 1, 2, False)]


class Level:
    def __init__(self, level, block):
        self.index = level
        self.rows, self.cols = block
        self.rim = RIM[level]
        self.high = self.rows + 2 * self.rim
        self.pitch = self.cols + 2 * self.rim
        self.store = self.high + 1
        while self.store * self.pitch % 8:
            self.store += 1
        known_rows, known_cols = KNOWN[level]
        self.pad_rows = known_rows + (self.rows if level >= 3 else 0)
        self.pad_cols = known_cols + (self.cols if level >= 4 else 0)
        self.stage_rows = self.rows + 2 * self.pad_rows
        self.stage_pitch = -(-(self.cols + 2 * self.pad_cols) // 8) * 8
        self.cuts = (pieces(level, self.rows, 0), pieces(level, self.cols, 1))
        received = sum(n for d, s, n, w in self.cuts[0]) * sum(n for d, s, n, w in self.cuts[1])
        own = [n for d, s, n, w in self.cuts[0] if d == 0][0] * [n for d, s, n, w in self.cuts[1] if d == 0][0]
        assert received == self.high * self.pitch
        self.arriving = received - own

    def span(self, depth):
        return depth * self.pitch + depth, (self.high - depth - 1) * self.pitch + self.pitch - depth


def blocks(first, last, body, chunk=CHUNK):
    count = last - first
    chunk = min(chunk, count)
    steps = -(-count // chunk)
    if steps <= 2:
        for step in range(steps):
            body(min(first + step * chunk, last - chunk), chunk)
        return

    def one(step, carry):
        body(jnp.minimum(first + step * chunk, last - chunk), chunk)
        return carry

    lax.fori_loop(0, steps, one, 0)


def lanes(shape):
    return lax.broadcasted_iota(jnp.int32, shape, 1)


def from_below(v):
    return jnp.where(lanes(v.shape) == 0, 0.0, pltpu.roll(v, 1, 1))


def from_above(v):
    return jnp.where(lanes(v.shape) == NZ - 1, 0.0, pltpu.roll(v, NZ - 1, 1))


def stencil_at(src, weight, pitch, row, rows):
    sums = [None, None, None]
    for a in range(3):
        for b in range(3):
            v = src[pl.ds(row + (a - 1) * pitch + b - 1, rows), :]
            for c in range(3):
                term = weight(9 * a + 3 * b + c) * v
                sums[c] = term if sums[c] is None else sums[c] + term
    return sums[1] + from_below(sums[0]) + from_above(sums[2])


def operate_at(src, diag, pitch, row, rows):
    v = src[pl.ds(row, rows), :]
    beside = (src[pl.ds(row - pitch, rows), :] + src[pl.ds(row + pitch, rows), :]) + (
        src[pl.ds(row - 1, rows), :] + src[pl.ds(row + 1, rows), :]
    )
    return diag[pl.ds(row, rows), :] * v - (beside + (from_below(v) + from_above(v)))


def smooth(dst, src, weight, lv, depth, mask=None, add=None):
    def body(row, rows):
        value = stencil_at(src, weight, lv.pitch, row, rows)
        if add is not None:
            value = value + add[pl.ds(row, rows), :]
        if mask is not None:
            value = value * mask[pl.ds(row, rows), :]
        dst[pl.ds(row, rows), :] = value

    blocks(*lv.span(depth), body)


def remain(dst, src, field, diag, mask, lv, depth):
    def body(row, rows):
        value = src[pl.ds(row, rows), :] - operate_at(field, diag, lv.pitch, row, rows)
        dst[pl.ds(row, rows), :] = value * mask[pl.ds(row, rows), :]

    blocks(*lv.span(depth), body)


def restrict(stage, fine, lv, below):
    known_rows, known_cols = KNOWN[below.index]
    first = -known_cols
    starts = range(first, below.cols + known_cols, 8)

    def body(step, carry):
        for start in starts:
            row = (lv.rim + 2 * (step - known_rows)) * lv.pitch + lv.rim + 2 * start
            total = (fine[pl.ds(row, 8, stride=2), :] + fine[pl.ds(row + 1, 8, stride=2), :]) + (
                fine[pl.ds(row + lv.pitch, 8, stride=2), :] + fine[pl.ds(row + lv.pitch + 1, 8, stride=2), :]
            )
            at = (below.pad_rows - known_rows + step) * below.stage_pitch + below.pad_cols + start
            width = min(8, below.cols + known_cols - start)
            stage[pl.ds(at, width), :] = 0.25 * total[:width]
        return carry

    count = below.rows + 2 * known_rows
    if count <= 4:
        for step in range(count):
            body(step, 0)
    else:
        lax.fori_loop(0, count, body, 0)


def prolong_onto(dst, base, coarse, lv, below):
    half = 1 if lv.index == 0 else 2
    first, last = -half, below.cols + half
    starts = []
    start = first
    while True:
        if last - start <= 8:
            starts.append(max(first, last - 8))
            break
        starts.append(start)
        start += 8

    def body(step, carry):
        line = step - half
        values = [
            coarse[pl.ds((below.rim + line) * below.pitch + below.rim + start, 8), :] for start in starts
        ]
        for part in range(2):
            for start, value in zip(starts, values):
                row = (lv.rim + 2 * line + part) * lv.pitch + lv.rim + 2 * start
                for side in range(2):
                    where = pl.ds(row + side, 8, stride=2)
                    dst[where, :] = base[where, :] + value
        return carry

    count = below.rows + 2 * half
    lax.fori_loop(0, count, body, 0)


def folded(v):
    rows = v.shape[0]
    total = v[0:8]
    for at in range(8, rows, 8):
        total = total + v[at : at + 8]
    return total


def products(cot, cot_first, cot_pitch, field, lv, totals=None):
    width = max(8, lv.cols)
    keep = None
    if lv.cols < 8:
        keep = lax.broadcasted_iota(jnp.int32, (8, NZ), 0) < lv.cols

    def body(step, totals):
        here = cot[pl.ds(cot_first + step * cot_pitch, width), :]
        if keep is not None:
            here = jnp.where(keep, here, 0.0)
        turned = (from_above(here), here, from_below(here))
        out = []
        for a in range(3):
            for b in range(3):
                v = field[pl.ds((lv.rim + step + a - 1) * lv.pitch + lv.rim + b - 1, width), :]
                for c in range(3):
                    out.append(totals[len(out)] + folded(turned[c] * v))
        return tuple(out)

    if totals is None:
        totals = tuple(jnp.zeros((8, NZ), jnp.float32) for _ in range(27))
    if lv.rows <= 2:
        for step in range(lv.rows):
            totals = body(step, totals)
        return totals
    return lax.fori_loop(0, lv.rows, body, totals)


def keep_sums(sums, totals, row):
    for entry, total in enumerate(totals):
        sums[pl.ds(row * 32 + entry, 1), :] = jnp.sum(total, axis=0, keepdims=True)


def kernel(gx_size, gy_size, lvs, rhs, target, stencils, walls, solution_out, grad_out, weights_out, *scratch):
    scratch = list(scratch)
    take = lambda: scratch.pop(0)
    src = [[take() for _ in lvs] for _ in range(2)]
    aft = [[take() for _ in lvs] for _ in range(2)]
    pre = [take() for _ in lvs]
    mid = [take() for _ in lvs]
    out = [take() for _ in lvs]
    mask = [take() for _ in lvs]
    diag = [take() for _ in lvs]
    stage = [take() for _ in lvs]
    last_rest = [take() for _ in range(2)]
    goal, result, grad, sums, mine, over_y, over_x = (take() for _ in range(7))
    recv, send, local, io, reduce_send, reduce_recv = (take() for _ in range(6))

    gx, gy = lax.axis_index("gx"), lax.axis_index("gy")

    def flat(ref, lv):
        return ref.reshape(2 * lv.stage_rows * lv.stage_pitch, NZ)

    stages = [flat(stage[i], lv) for i, lv in enumerate(lvs)]
    blocks3 = [[src[way][i].reshape(lv.store, lv.pitch, NZ) for i, lv in enumerate(lvs)] for way in range(2)]

    def device(x, y):
        return (lax.rem(x + 2 * gx_size, gx_size), lax.rem(y + 2 * gy_size, gy_size))

    load_target = pltpu.make_async_copy(target, goal, io.at[0])
    load_target.start()
    for i, lv in enumerate(lvs):
        rows = lv.stage_rows * lv.stage_pitch
        first = rows if i < 2 else 0

        def clear(row, count, i=i):
            stages[i][pl.ds(row, count), :] = jnp.zeros((count, NZ), jnp.float32)

        blocks(first, 2 * rows, clear)
    load_rhs = pltpu.make_async_copy(rhs, stage[0].at[0], io.at[1])
    load_rhs.start()

    barrier = pltpu.get_barrier_semaphore()
    near = [(d, e) for d in (-2, -1, 0, 1, 2) for e in (-1, 0, 1) if (d, e) != (0, 0)]
    near = sorted(set((d % gx_size, e % gy_size) for d, e in near))
    for d, e in near:
        pl.semaphore_signal(barrier, inc=1, device_id=device(gx + d, gy + e), device_id_type=MESH)

    def lay_out(i):
        lv = lvs[i]
        wall = [walls[k].astype(jnp.float32) for k in range(6)]
        total_rows, total_cols = gx_size * lv.rows, gy_size * lv.cols
        starts = list(range(0, lv.pitch, 8))

        def body(step, carry):
            line = gx * lv.rows - lv.rim + step
            first = jnp.where(line == 0, wall[0], 0.0) + jnp.where(line == total_rows - 1, wall[1], 0.0)
            within = (line >= 0) & (line < total_rows)
            for start in starts:
                column = gy * lv.cols - lv.rim + start + lax.broadcasted_iota(jnp.int32, (8, NZ), 0)
                lane = lanes((8, NZ))
                tally = first + jnp.where(column == 0, wall[2], 0.0) + jnp.where(column == total_cols - 1, wall[3], 0.0)
                tally = tally + jnp.where(lane == 0, wall[4], 0.0) + jnp.where(lane == NZ - 1, wall[5], 0.0)
                inside = (column >= 0) & (column < total_cols) & within
                where = pl.ds(step * lv.pitch + start, 8)
                diag[i][where, :] = 6.0 - tally
                mask[i][where, :] = jnp.where(inside, 1.0, 0.0)
            return carry

        lax.fori_loop(0, lv.high, body, 0)

    def placed(cut, me, size, block, known):
        offset, first, count, inward = cut
        if inward:
            low = offset > 0
            swapped = (me == 0) if low else (me == size - 1)
            step = -1 if low else 1
            acting = jnp.where(swapped, me + step, me)
            mirrored = jnp.where(swapped, -offset, offset)
            other = block - first - count
            begin = jnp.where(swapped, other + step * block, first)
            start = jnp.where(swapped, other, first)
        else:
            acting, mirrored, begin, start = me, offset, first, first
        to = acting - mirrored
        outside = (to < 0) | (to >= size)
        return begin, to, mirrored * block + start, outside, count

    def exchange(way, i):
        lv = lvs[i]
        for cut_x in lv.cuts[0]:
            begin_x, to_x, land_x, out_x, count_x = placed(cut_x, gx, gx_size, lv.rows, 0)
            for cut_y in lv.cuts[1]:
                begin_y, to_y, land_y, out_y, count_y = placed(cut_y, gy, gy_size, lv.cols, 0)
                dst = blocks3[way][i].at[pl.ds(lv.rim + land_x, count_x), pl.ds(lv.rim + land_y, count_y)]
                if cut_x[0] == 0 and cut_y[0] == 0:
                    piece = stage[i].at[
                        0, pl.ds(lv.pad_rows + begin_x, count_x), pl.ds(lv.pad_cols + begin_y, count_y)
                    ]
                    pltpu.make_async_copy(piece, dst, local.at[way, i]).start()
                    continue
                piece = stage[i].at[
                    jnp.where(out_x | out_y, 1, 0),
                    pl.ds(lv.pad_rows + begin_x, count_x),
                    pl.ds(lv.pad_cols + begin_y, count_y),
                ]
                pltpu.make_async_remote_copy(
                    src_ref=piece,
                    dst_ref=dst,
                    send_sem=send.at[way, i],
                    recv_sem=recv.at[way, i],
                    device_id=device(to_x, to_y),
                    device_id_type=MESH,
                ).start()

    def await_bytes(ref, rows, sem):
        pltpu.make_async_copy(ref.at[pl.ds(0, rows)], ref.at[pl.ds(0, rows)], sem).wait()

    def arrived(way, i):
        lv = lvs[i]
        await_bytes(src[way][i], lv.arriving, recv.at[way, i])
        await_bytes(src[way][i], lv.high * lv.pitch - lv.arriving, local.at[way, i])

    def sent(way, i):
        await_bytes(src[way][i], lvs[i].arriving, send.at[way, i])

    def weights(way, row):
        if way == 0:
            return lambda entry: stencils[row, entry]
        return lambda entry: stencils[row, 26 - entry]

    def cycle(way, waiting):
        for i in range(LEVELS):
            lv = lvs[i]
            exchange(way, i)
            waiting(i)
            arrived(way, i)
            smooth(pre[i], src[way][i], weights(way, i if way == 0 else LEVELS + i), lv, 1, mask[i])
            known = max(KNOWN[i + 1])
            remain(mid[i], src[way][i], pre[i], diag[i], mask[i], lv, lv.rim - 2 * known)
            sent(way, i)
            if way == 1 and i + 1 == LEVELS:
                sent(0, LEVELS)
            restrict(stages[i + 1], mid[i], lv, lvs[i + 1])
        bottom = lvs[LEVELS]
        weight = weights(way, 2 * LEVELS)
        exchange(way, LEVELS)
        waiting(LEVELS)
        arrived(way, LEVELS)
        b = src[way][LEVELS]
        x, y = pre[LEVELS], mid[LEVELS]
        rest = (aft[way][LEVELS], last_rest[way])
        smooth(x, b, weight, bottom, 1, mask[LEVELS])
        remain(rest[0], b, x, diag[LEVELS], mask[LEVELS], bottom, 2)
        smooth(y, rest[0], weight, bottom, 3, mask[LEVELS], x)
        remain(rest[1], b, y, diag[LEVELS], mask[LEVELS], bottom, 4)
        smooth(out[LEVELS], rest[1], weight, bottom, 5, mask[LEVELS], y)
        if way == 1:
            sent(1, LEVELS)
        for i in reversed(range(LEVELS)):
            lv = lvs[i]
            prolong_onto(mid[i], pre[i], out[i + 1], lv, lvs[i + 1])
            remain(aft[way][i], src[way][i], mid[i], diag[i], mask[i], lv, 2)
            if i > 0:
                smooth(out[i], aft[way][i], weights(way, LEVELS + i if way == 0 else i), lv, 3, mask[i], mid[i])

    def finish(weight, way, store):
        lv = lvs[0]

        def body(step, carry):
            row = (lv.rim + step) * lv.pitch + lv.rim
            value = stencil_at(aft[way][0], weight, lv.pitch, row, lv.cols)
            store(step, value + mid[0][pl.ds(row, lv.cols), :])
            return carry

        lax.fori_loop(0, lv.rows, body, 0)

    lay_out(0)
    load_rhs.wait()
    pl.semaphore_wait(barrier, len(near))

    def forward_waits(i):
        if i == 0:
            for level in range(1, LEVELS + 1):
                lay_out(level)
            rows = sums.shape[0]
            sums[...] = jnp.zeros((rows, NZ), jnp.float32)

    cycle(0, forward_waits)

    load_target.wait()

    def store_solution(step, value):
        result[step] = value
        stage[0][0, step] = value - goal[step]

    finish(weights(0, LEVELS), 0, store_solution)
    save_solution = pltpu.make_async_copy(result, solution_out, io.at[2])
    save_solution.start()

    def backward_waits(i):
        lv = lvs[i]
        if i < LEVELS:
            first = lv.pad_rows * lv.stage_pitch + lv.pad_cols
            keep_sums(sums, products(stages[i], first, lv.stage_pitch, aft[0][i], lv), LEVELS + i)

    cycle(1, backward_waits)

    bottom = lvs[LEVELS]
    at = bottom.rim * bottom.pitch + bottom.rim
    totals = products(src[1][LEVELS], at, bottom.pitch, last_rest[0], bottom)
    totals = products(aft[1][LEVELS], at, bottom.pitch, aft[0][LEVELS], bottom, totals)
    totals = products(last_rest[1], at, bottom.pitch, src[0][LEVELS], bottom, totals)
    keep_sums(sums, totals, 2 * LEVELS)
    for i in reversed(range(LEVELS)):
        lv = lvs[i]
        at = lv.rim * lv.pitch + lv.rim
        keep_sums(sums, products(aft[1][i], at, lv.pitch, src[0][i], lv), i)

    ones = jnp.ones((8, NZ), jnp.float32)
    for part in range(3):
        line = lax.dot_general(
            ones,
            sums[pl.ds(part * NZ, NZ), :],
            (((1,), (1,)), ((), ())),
            precision=lax.Precision.HIGHEST,
            preferred_element_type=jnp.float32,
        )
        mine[0, pl.ds(part, 1), :] = line[0:1]

    def spread(slot, held, me, size, where):
        source = mine.at[slot, pl.ds(0, 3)]
        for step in range(1, size):
            pltpu.make_async_remote_copy(
                src_ref=source,
                dst_ref=held.at[me, pl.ds(0, 3)],
                send_sem=reduce_send.at[slot],
                recv_sem=reduce_recv.at[slot],
                device_id=where(step),
                device_id_type=MESH,
            ).start()
        held[me] = mine[slot]

    def gathered(slot, held, size):
        await_bytes(src[0][0], 3 * (size - 1), reduce_recv.at[slot])
        total = held[0]
        for step in range(1, size):
            total = total + held[step]
        return total

    spread(0, over_y, gy, gy_size, lambda step: device(gx, gy + step))

    def store_grad(step, value):
        grad[step] = value

    finish(weights(1, 0), 1, store_grad)
    save_grad = pltpu.make_async_copy(grad, grad_out, io.at[3])
    save_grad.start()

    mine[1] = gathered(0, over_y, gy_size)
    spread(1, over_x, gx, gx_size, lambda step: device(gx + step, gy))
    await_bytes(src[0][0], 3 * (gy_size - 1), reduce_send.at[0])
    save_solution.wait()
    save_grad.wait()
    total = gathered(1, over_x, gx_size)
    await_bytes(src[0][0], 3 * (gx_size - 1), reduce_send.at[1])
    cells = gx_size * lvs[0].rows * gy_size * lvs[0].cols * NZ
    for row in range(2 * LEVELS + 1):
        scale = SCALES[row % LEVELS if row < 2 * LEVELS else LEVELS] / cells
        part, lane = row // 4, 32 * (row % 4)
        weights_out[pl.ds(row, 1), :] = total[part : part + 1, lane : lane + 27] * scale


def on_device(gx_size, gy_size, rhs, target, stencils, face_mask):
    rows, cols, _ = rhs.shape
    lvs = [Level(i, (rows >> i, cols >> i)) for i in range(LEVELS + 1)]
    field = lambda lv: pltpu.VMEM((lv.store * lv.pitch, NZ), jnp.float32)
    scratch = []
    for _ in range(9):
        scratch += [field(lv) for lv in lvs]
    scratch += [pltpu.VMEM((2, lv.stage_rows, lv.stage_pitch, NZ), jnp.float32) for lv in lvs]
    scratch += [field(lvs[LEVELS])] * 2
    scratch += [pltpu.VMEM((rows, cols, NZ), jnp.float32)] * 3
    scratch += [
        pltpu.VMEM((3 * NZ, NZ), jnp.float32),
        pltpu.VMEM((2, 8, NZ), jnp.float32),
        pltpu.VMEM((gy_size, 8, NZ), jnp.float32),
        pltpu.VMEM((gx_size, 8, NZ), jnp.float32),
        pltpu.SemaphoreType.DMA((2, LEVELS + 1)),
        pltpu.SemaphoreType.DMA((2, LEVELS + 1)),
        pltpu.SemaphoreType.DMA((2, LEVELS + 1)),
        pltpu.SemaphoreType.DMA((4,)),
        pltpu.SemaphoreType.DMA((2,)),
        pltpu.SemaphoreType.DMA((2,)),
    ]
    return pl.pallas_call(
        functools.partial(kernel, gx_size, gy_size, lvs),
        out_shape=(
            jax.ShapeDtypeStruct(rhs.shape, jnp.float32),
            jax.ShapeDtypeStruct(rhs.shape, jnp.float32),
            jax.ShapeDtypeStruct(stencils.shape, jnp.float32),
        ),
        in_specs=[
            pl.BlockSpec(memory_space=pl.ANY),
            pl.BlockSpec(memory_space=pl.ANY),
            pl.BlockSpec(memory_space=pltpu.SMEM),
            pl.BlockSpec(memory_space=pltpu.SMEM),
        ],
        out_specs=(
            pl.BlockSpec(memory_space=pl.ANY),
            pl.BlockSpec(memory_space=pl.ANY),
            pl.BlockSpec(memory_space=pltpu.VMEM),
        ),
        scratch_shapes=scratch,
        compiler_params=pltpu.CompilerParams(
            collective_id=0, has_side_effects=True, vmem_limit_bytes=40 << 20
        ),
        cost_estimate=pl.CostEstimate(flops=60_000_000, bytes_accessed=1_100_000, transcendentals=0),
    )(rhs, target, stencils, face_mask)


def solution(mesh):
    sizes = dict(mesh.shape)
    return jax.shard_map(
        functools.partial(on_device, sizes["gx"], sizes["gy"]),
        mesh=mesh,
        in_specs=(P("gx", "gy", None), P("gx", "gy", None), P(), P()),
        out_specs=(P("gx", "gy", None), P("gx", "gy", None), P()),
        check_vma=False,
    )
```

time: 1190 us -> 106 us (0.09); the launches traced: 1160 us -> 106 us
  other arithmetic: 459 us -> 0 us
  starting transfers between devices: 292 us -> 0 us
  local copies, waits for them, and re-layouts: 219 us -> 5.25 us
  waiting for transfers between devices: 101 us -> 0 us
  Pallas kernels: 0 us -> 99.8 us
  blocking collectives: 88.7 us -> 0 us
    ppermute x100 -> x0, starting transfers between devices: 278 us -> none  [the longest x50 189 us: extended(): before = lax.ppermute(last, axis, up)]
    mul x27 -> x0, other arithmetic: 215 us -> none  [the longest x8 144 us: smooth_then_apply(): smoothed_loop = shifted_sum(deep, weights, wider) * loop_inside(shape)]
    another operation x12 -> x0, local copies, waits for them, and re-layouts: 187 us -> none  [the longest x11 187 us: weight_sums(): return jnp.stack(sums)]
    add x23 -> x0, other arithmetic: 178 us -> none  [the longest x5 81 us: shifted_sum(): total + weights[9 * shift_first + 3 * shift_second + shift_third] * window]
    pallas_call x0 -> x1, Pallas kernels: none -> 99.8 us  [on_device(): pl.pallas_call(functools.partial(kernel, gx_size, gy_size, lvs), out_shap...]
    ppermute x100 -> x0, waiting for transfers between devices: 93.4 us -> none  [the longest x50 92.4 us: extended(): after = lax.ppermute(initial, axis, down)]
    psum x4 -> x0, blocking collectives: 67.1 us -> none  [one_axis_at_a_time(): array = lax.psum(array, axis)]
    reduce_sum x32 -> x0, other arithmetic: 48.1 us -> none  [the longest x22 42.3 us: weight_sums(): sums.append(jnp.sum(cotangent * window))]
  transfers between devices with their start and end apart: 101 -> 0, of which waited for: 35 -> 0; matrix products, arithmetic and copies ran while one was open for 21% -> 0% of each run, Pallas kernels for 0% -> 0%
where the time goes in v1:
time: 106 us
  Pallas kernels  99.8 us (94%)
  local copies, waits for them, and re-layouts  5.25 us (5%)
    pallas_call x1, Pallas kernels, on_device(): pl.pallas_call(functools.partial(kernel, gx_size, gy_size, lvs), out_shap...  99.8 us
    unnamed x11, local copies, waits for them, and re-layouts  5.25 us

profile of v1, /device:TPU:1, one launch (start us, length us, event | category | flops | bytes accessed | tf_op | source)
XLA Modules:
  0.0 105.7 jit_solution(9527620454977074248)
XLA Ops:
  0.6 0.0 copy-start
  0.6 0.9 copy-done
  1.6 0.0 copy-start.1
  1.6 0.9 copy-done.1
  2.5 0.0 copy-start.2
  2.5 0.7 copy-done.2
  3.2 0.0 copy-start.3
  3.2 0.7 copy-done.3
  3.9 99.8 %shard_map.67 = (f32[16,32,128]{2,1,0:T(8,128)S(1)}, f32[16,32,128]{2,1,0:T(8,128)S(1)}, f32[9,27]{1,0:T(8,128)S(1)}) custom-call(f32[16,32,128]{2,1,0:T(8,128)S(1)} %copy-done, f32[16,32,128]{2,1,0:T(8,128)S(1)} %copy-done.1, f32[9,27]{1,0:T(8,128)S(1)} %copy-done.2, s32[6]{0:T(128)S(1)} %copy-done.3), custom_call_target="tpu_custom_call" | custom-call | flops 60000000 | bytes 1100000 | tf_op jit(solution)/shard_map/pallas_call | solution.py:514
  103.7 0.7 copy.10
  104.4 0.7 copy.11
  105.1 0.6 copy.12
Async XLA Ops:
  0.6 1.0 copy-start
  1.6 0.9 copy-start.1
  2.5 0.7 copy-start.2
  3.2 0.7 copy-start.3

commit v2 on v1

--- a/solution.py
+++ b/solution.py
@@ -10,7 +10,8 @@
 MESH = pl.DeviceIdType.MESH
 LEVELS = 4
 NZ = 128
-CHUNK = 64
+CHUNK = 384
+UNROLL = 8
 RIM = (3, 4, 5, 5, 7)
 KNOWN = ((0, 0), (0, 0), (1, 0), (1, 1), (1, 1))
 SCALES = tuple(4.0**level for level in range(LEVELS + 1))
@@ -74,6 +75,14 @@
     lax.fori_loop(0, steps, one, 0)
 
 
+def hops_x(offset):
+    return min(abs(offset), 8 - abs(offset)) + (offset != 0)
+
+
+def hops_y(offset):
+    return abs(offset) / 2
+
+
 def lanes(shape):
     return lax.broadcasted_iota(jnp.int32, shape, 1)
 
@@ -211,7 +220,14 @@
         for step in range(lv.rows):
             totals = body(step, totals)
         return totals
-    return lax.fori_loop(0, lv.rows, body, totals)
+    unroll = min(UNROLL, lv.rows)
+
+    def several(step, totals):
+        for part in range(unroll):
+            totals = body(step * unroll + part, totals)
+        return totals
+
+    return lax.fori_loop(0, lv.rows // unroll, several, totals)
 
 
 def keep_sums(sums, totals, row):
@@ -219,7 +235,7 @@
         sums[pl.ds(row * 32 + entry, 1), :] = jnp.sum(total, axis=0, keepdims=True)
 
 
-def kernel(gx_size, gy_size, lvs, rhs, target, stencils, walls, solution_out, grad_out, weights_out, *scratch):
+def kernel(gx_size, gy_size, lvs, rhs, target, stencils_in, walls_in, solution_out, grad_out, weights_out, *scratch):
     scratch = list(scratch)
     take = lambda: scratch.pop(0)
     src = [[take() for _ in lvs] for _ in range(2)]
@@ -232,6 +248,7 @@
     stage = [take() for _ in lvs]
     last_rest = [take() for _ in range(2)]
     goal, result, grad, sums, mine, over_y, over_x = (take() for _ in range(7))
+    stencils, walls = take(), take()
     recv, send, local, io, reduce_send, reduce_recv = (take() for _ in range(6))
 
     gx, gy = lax.axis_index("gx"), lax.axis_index("gy")
@@ -247,6 +264,10 @@
 
     load_target = pltpu.make_async_copy(target, goal, io.at[0])
     load_target.start()
+    load_walls = pltpu.make_async_copy(walls_in, walls, io.at[4])
+    load_walls.start()
+    load_stencils = pltpu.make_async_copy(stencils_in, stencils, io.at[5])
+    load_stencils.start()
     for i, lv in enumerate(lvs):
         rows = lv.stage_rows * lv.stage_pitch
         first = rows if i < 2 else 0
@@ -287,7 +308,7 @@
 
         lax.fori_loop(0, lv.high, body, 0)
 
-    def placed(cut, me, size, block, known):
+    def placed(cut, me, size, block):
         offset, first, count, inward = cut
         if inward:
             low = offset > 0
@@ -306,30 +327,34 @@
 
     def exchange(way, i):
         lv = lvs[i]
-        for cut_x in lv.cuts[0]:
-            begin_x, to_x, land_x, out_x, count_x = placed(cut_x, gx, gx_size, lv.rows, 0)
-            for cut_y in lv.cuts[1]:
-                begin_y, to_y, land_y, out_y, count_y = placed(cut_y, gy, gy_size, lv.cols, 0)
-                dst = blocks3[way][i].at[pl.ds(lv.rim + land_x, count_x), pl.ds(lv.rim + land_y, count_y)]
-                if cut_x[0] == 0 and cut_y[0] == 0:
-                    piece = stage[i].at[
-                        0, pl.ds(lv.pad_rows + begin_x, count_x), pl.ds(lv.pad_cols + begin_y, count_y)
-                    ]
-                    pltpu.make_async_copy(piece, dst, local.at[way, i]).start()
-                    continue
+        across = [placed(cut, gx, gx_size, lv.rows) for cut in lv.cuts[0]]
+        along = [placed(cut, gy, gy_size, lv.cols) for cut in lv.cuts[1]]
+        pairs = [(p, q) for p in range(len(across)) for q in range(len(along))]
+        pairs.sort(key=lambda pq: -(hops_x(lv.cuts[0][pq[0]][0]) + hops_y(lv.cuts[1][pq[1]][0])))
+        for p, q in pairs:
+            cut_x, cut_y = lv.cuts[0][p], lv.cuts[1][q]
+            begin_x, to_x, land_x, out_x, count_x = across[p]
+            begin_y, to_y, land_y, out_y, count_y = along[q]
+            dst = blocks3[way][i].at[pl.ds(lv.rim + land_x, count_x), pl.ds(lv.rim + land_y, count_y)]
+            if cut_x[0] == 0 and cut_y[0] == 0:
                 piece = stage[i].at[
-                    jnp.where(out_x | out_y, 1, 0),
-                    pl.ds(lv.pad_rows + begin_x, count_x),
-                    pl.ds(lv.pad_cols + begin_y, count_y),
+                    0, pl.ds(lv.pad_rows + begin_x, count_x), pl.ds(lv.pad_cols + begin_y, count_y)
                 ]
-                pltpu.make_async_remote_copy(
-                    src_ref=piece,
-                    dst_ref=dst,
-                    send_sem=send.at[way, i],
-                    recv_sem=recv.at[way, i],
-                    device_id=device(to_x, to_y),
-                    device_id_type=MESH,
-                ).start()
+                pltpu.make_async_copy(piece, dst, local.at[way, i]).start()
+                continue
+            piece = stage[i].at[
+                jnp.where(out_x | out_y, 1, 0),
+                pl.ds(lv.pad_rows + begin_x, count_x),
+                pl.ds(lv.pad_cols + begin_y, count_y),
+            ]
+            pltpu.make_async_remote_copy(
+                src_ref=piece,
+                dst_ref=dst,
+                send_sem=send.at[way, i],
+                recv_sem=recv.at[way, i],
+                device_id=device(to_x, to_y),
+                device_id_type=MESH,
+            ).start()
 
     def await_bytes(ref, rows, sem):
         pltpu.make_async_copy(ref.at[pl.ds(0, rows)], ref.at[pl.ds(0, rows)], sem).wait()
@@ -386,14 +411,18 @@
         lv = lvs[0]
 
         def body(step, carry):
-            row = (lv.rim + step) * lv.pitch + lv.rim
-            value = stencil_at(aft[way][0], weight, lv.pitch, row, lv.cols)
-            store(step, value + mid[0][pl.ds(row, lv.cols), :])
+            for part in range(UNROLL):
+                line = step * UNROLL + part
+                row = (lv.rim + line) * lv.pitch + lv.rim
+                value = stencil_at(aft[way][0], weight, lv.pitch, row, lv.cols)
+                store(line, value + mid[0][pl.ds(row, lv.cols), :])
             return carry
 
-        lax.fori_loop(0, lv.rows, body, 0)
-
+        lax.fori_loop(0, lv.rows // UNROLL, body, 0)
+
+    load_walls.wait()
     lay_out(0)
+    load_stencils.wait()
     load_rhs.wait()
     pl.semaphore_wait(barrier, len(near))
 
@@ -446,9 +475,9 @@
         )
         mine[0, pl.ds(part, 1), :] = line[0:1]
 
-    def spread(slot, held, me, size, where):
+    def spread(slot, held, me, order, where):
         source = mine.at[slot, pl.ds(0, 3)]
-        for step in range(1, size):
+        for step in order:
             pltpu.make_async_remote_copy(
                 src_ref=source,
                 dst_ref=held.at[me, pl.ds(0, 3)],
@@ -466,7 +495,8 @@
             total = total + held[step]
         return total
 
-    spread(0, over_y, gy, gy_size, lambda step: device(gx, gy + step))
+    order = sorted(range(1, gy_size), key=lambda step: -min(step, gy_size - step))
+    spread(0, over_y, gy, order, lambda step: device(gx, gy + step))
 
     def store_grad(step, value):
         grad[step] = value
@@ -476,7 +506,8 @@
     save_grad.start()
 
     mine[1] = gathered(0, over_y, gy_size)
-    spread(1, over_x, gx, gx_size, lambda step: device(gx + step, gy))
+    order = sorted(range(1, gx_size), key=lambda step: -min(step % 8, 8 - step % 8) - min(step, gx_size - step) / 8)
+    spread(1, over_x, gx, order, lambda step: device(gx + step, gy))
     await_bytes(src[0][0], 3 * (gy_size - 1), reduce_send.at[0])
     save_solution.wait()
     save_grad.wait()
@@ -504,10 +535,12 @@
         pltpu.VMEM((2, 8, NZ), jnp.float32),
         pltpu.VMEM((gy_size, 8, NZ), jnp.float32),
         pltpu.VMEM((gx_size, 8, NZ), jnp.float32),
+        pltpu.SMEM(stencils.shape, jnp.float32),
+        pltpu.SMEM(face_mask.shape, jnp.int32),
         pltpu.SemaphoreType.DMA((2, LEVELS + 1)),
         pltpu.SemaphoreType.DMA((2, LEVELS + 1)),
         pltpu.SemaphoreType.DMA((2, LEVELS + 1)),
-        pltpu.SemaphoreType.DMA((4,)),
+        pltpu.SemaphoreType.DMA((6,)),
         pltpu.SemaphoreType.DMA((2,)),
         pltpu.SemaphoreType.DMA((2,)),
     ]
@@ -519,10 +552,10 @@
             jax.ShapeDtypeStruct(stencils.shape, jnp.float32),
         ),
         in_specs=[
-            pl.BlockSpec(memory_space=pl.ANY),
-            pl.BlockSpec(memory_space=pl.ANY),
-            pl.BlockSpec(memory_space=pltpu.SMEM),
-            pl.BlockSpec(memory_space=pltpu.SMEM),
+            pl.BlockSpec(memory_space=pltpu.HBM),
+            pl.BlockSpec(memory_space=pltpu.HBM),
+            pl.BlockSpec(memory_space=pltpu.HBM),
+            pl.BlockSpec(memory_space=pltpu.HBM),
         ],
         out_specs=(
             pl.BlockSpec(memory_space=pl.ANY),
@@ -531,7 +564,7 @@
         ),
         scratch_shapes=scratch,
         compiler_params=pltpu.CompilerParams(
-            collective_id=0, has_side_effects=True, vmem_limit_bytes=40 << 20
+            collective_id=0, has_side_effects=True, vmem_limit_bytes=60 << 20
         ),
         cost_estimate=pl.CostEstimate(flops=60_000_000, bytes_accessed=1_100_000, transcendentals=0),
     )(rhs, target, stencils, face_mask)

time: 106 us -> 89.4 us (0.84)
  Pallas kernels: 99.8 us -> 85.5 us
  local copies, waits for them, and re-layouts: 5.25 us -> 3.02 us
    pallas_call x1, Pallas kernels: 99.8 us -> 85.5 us  [on_device(): pl.pallas_call(functools.partial(kernel, gx_size, gy_size, lvs), out_shap...]
    unnamed x11 -> x7, local copies, waits for them, and re-layouts: 5.25 us -> 3.02 us
where the time goes in v2:
time: 89.4 us; the launch traced here: 89.2 us
  Pallas kernels  85.5 us (96%)
  local copies, waits for them, and re-layouts  3.02 us (3%)
    pallas_call x1, Pallas kernels, on_device(): pl.pallas_call(functools.partial(kernel, gx_size, gy_size, lvs), out_shap...  85.5 us
    unnamed x7, local copies, waits for them, and re-layouts  3.02 us

profile of v2, /device:TPU:1, one launch (start us, length us, event | category | flops | bytes accessed | tf_op | source)
XLA Modules:
  0.0 89.2 jit_solution(2063562554324873244)
XLA Ops:
  0.6 85.5 %shard_map.67 = (f32[16,32,128]{2,1,0:T(8,128)}, f32[16,32,128]{2,1,0:T(8,128)}, f32[9,27]{1,0:T(8,128)}) custom-call(f32[16,32,128]{2,1,0:T(8,128)} %rhs.1, f32[16,32,128]{2,1,0:T(8,128)} %target.1, f32[9,27]{1,0:T(8,128)} %stencils_in.1, s32[6]{0:T(128)} %walls_in.1), custom_call_target="tpu_custom_call" | custom-call | flops 60000000 | bytes 1100000 | tf_op jit(solution)/shard_map/pallas_call | solution.py:547
  86.2 0.0 copy-start
  86.2 1.7 %copy.10 = f32[16,32,128]{2,1,0:T(8,128)} copy(f32[16,32,128]{2,1,0:T(8,128)} %get-tuple-element.6) | data formatting | bytes 524288
  87.9 0.0 copy-done
  87.9 0.0 copy-start.1
  87.9 0.7 copy.11
  88.6 0.0 copy-done.1
  88.6 0.6 copy.12
Async XLA Ops:
  86.2 1.7 %copy-start = (f32[16,32,128]{2,1,0:T(8,128)S(1)}, f32[16,32,128]{2,1,0:T(8,128)}, u32[]{:S(2)}) copy-start(f32[16,32,128]{2,1,0:T(8,128)} %get-tuple-element.7) | copy-start | bytes 786436
  87.9 0.7 copy-start.1

commit v3 on v2

--- a/solution.py
+++ b/solution.py
@@ -12,46 +12,47 @@
 NZ = 128
 CHUNK = 384
 UNROLL = 8
-RIM = (3, 4, 5, 5, 7)
-KNOWN = ((0, 0), (0, 0), (1, 0), (1, 1), (1, 1))
+RIM = (3, 6, 6, 6, 8)
+WIDE = 6
+KNOWN = ((0, 0), (0, 0), (2, 0), (2, 2), (2, 2))
+LESS = (0, 2, 1, 1, 1)
 SCALES = tuple(4.0**level for level in range(LEVELS + 1))
 
 
-def pieces(level, block, axis):
-    rim = RIM[level]
+def pieces(level, block, axis, rim):
     if level <= 1:
-        return [(-1, block - rim, rim, False), (0, 0, block, False), (1, 0, rim, False)]
+        return [(-1, block - rim, rim), (0, 0, block), (1, 0, rim)]
     if level == 2:
         if axis == 0:
-            return [(-1, -1, 4, False), (0, -1, 6, False), (1, 1, 4, False)]
-        return [(-1, 3, 5, False), (0, 0, 8, False), (1, 0, 5, False)]
+            return [(-1, -2, 4), (0, -2, 8), (1, 2, 4)]
+        return [(-1, 2, 6), (0, 0, 8), (1, 0, 6)]
     if level == 3:
         if axis == 0:
-            return [(-2, -1, 4, True), (0, -1, 4, False), (2, -1, 4, True)]
-        return [(-1, -1, 4, False), (0, -1, 6, False), (1, 1, 4, False)]
+            return [(-2, -2, 4), (0, -2, 6), (2, 0, 4)]
+        return [(-1, -2, 4), (0, -2, 8), (1, 2, 4)]
     if axis == 0:
-        return [(d, -1, 3, d != 0) for d in (-6, -3, 0, 3, 6)]
-    return [(-3, -1, 2, False), (-2, -1, 4, True), (0, -1, 4, False), (2, -1, 4, True), (3, 1, 2, False)]
+        return [(-6, -2, 3), (-3, -2, 3), (0, -2, 5), (3, 0, 3), (6, 0, 3)]
+    return [(-3, -2, 2), (-2, -2, 4), (0, -2, 6), (2, 0, 4), (3, 2, 2)]
 
 
 class Level:
-    def __init__(self, level, block):
+    def __init__(self, level, block, rim):
         self.index = level
         self.rows, self.cols = block
-        self.rim = RIM[level]
+        self.rim = rim
         self.high = self.rows + 2 * self.rim
         self.pitch = self.cols + 2 * self.rim
         self.store = self.high + 1
         while self.store * self.pitch % 8:
             self.store += 1
         known_rows, known_cols = KNOWN[level]
-        self.pad_rows = known_rows + (self.rows if level >= 3 else 0)
-        self.pad_cols = known_cols + (self.cols if level >= 4 else 0)
+        self.pad_rows, self.pad_cols = known_rows, known_cols
+        self.slots = 3 if level == 0 else 2
         self.stage_rows = self.rows + 2 * self.pad_rows
         self.stage_pitch = -(-(self.cols + 2 * self.pad_cols) // 8) * 8
-        self.cuts = (pieces(level, self.rows, 0), pieces(level, self.cols, 1))
-        received = sum(n for d, s, n, w in self.cuts[0]) * sum(n for d, s, n, w in self.cuts[1])
-        own = [n for d, s, n, w in self.cuts[0] if d == 0][0] * [n for d, s, n, w in self.cuts[1] if d == 0][0]
+        self.cuts = (pieces(level, self.rows, 0, rim), pieces(level, self.cols, 1, rim))
+        received = sum(n for d, s, n in self.cuts[0]) * sum(n for d, s, n in self.cuts[1])
+        own = [n for d, s, n in self.cuts[0] if d == 0][0] * [n for d, s, n in self.cuts[1] if d == 0][0]
         assert received == self.high * self.pitch
         self.arriving = received - own
 
@@ -158,8 +159,7 @@
         lax.fori_loop(0, count, body, 0)
 
 
-def prolong_onto(dst, base, coarse, lv, below):
-    half = 1 if lv.index == 0 else 2
+def prolong_onto(dst, base, coarse, lv, below, half):
     first, last = -half, below.cols + half
     starts = []
     start = first
@@ -236,6 +236,7 @@
 
 
 def kernel(gx_size, gy_size, lvs, rhs, target, stencils_in, walls_in, solution_out, grad_out, weights_out, *scratch):
+    lvs, wide = lvs[: LEVELS + 1], lvs[LEVELS + 1]
     scratch = list(scratch)
     take = lambda: scratch.pop(0)
     src = [[take() for _ in lvs] for _ in range(2)]
@@ -247,46 +248,46 @@
     diag = [take() for _ in lvs]
     stage = [take() for _ in lvs]
     last_rest = [take() for _ in range(2)]
-    goal, result, grad, sums, mine, over_y, over_x = (take() for _ in range(7))
+    wide_src, wide_pre, wide_mid, wide_aft, wide_out, wide_mask, wide_diag = (take() for _ in range(7))
+    goal, grad, sums, mine, over_y, over_x = (take() for _ in range(6))
     stencils, walls = take(), take()
-    recv, send, local, io, reduce_send, reduce_recv = (take() for _ in range(6))
+    recv, send, local, io, reduce_send, reduce_recv, extra_send, extra_recv, extra_local = (take() for _ in range(9))
 
     gx, gy = lax.axis_index("gx"), lax.axis_index("gy")
 
     def flat(ref, lv):
-        return ref.reshape(2 * lv.stage_rows * lv.stage_pitch, NZ)
+        return ref.reshape(lv.slots * lv.stage_rows * lv.stage_pitch, NZ)
 
     stages = [flat(stage[i], lv) for i, lv in enumerate(lvs)]
     blocks3 = [[src[way][i].reshape(lv.store, lv.pitch, NZ) for i, lv in enumerate(lvs)] for way in range(2)]
+    grid3 = lambda ref, lv: ref.reshape(lv.store, lv.pitch, NZ)
 
     def device(x, y):
         return (lax.rem(x + 2 * gx_size, gx_size), lax.rem(y + 2 * gy_size, gy_size))
 
-    load_target = pltpu.make_async_copy(target, goal, io.at[0])
-    load_target.start()
+    barrier = pltpu.get_barrier_semaphore()
+    near = [(d, e) for d in (-1, 0, 1) for e in (-1, 0, 1) if (d, e) != (0, 0)]
+    for d, e in near:
+        pl.semaphore_signal(barrier, inc=1, device_id=device(gx + d, gy + e), device_id_type=MESH)
+    load_rhs = pltpu.make_async_copy(rhs, stage[0].at[0], io.at[1])
+    load_rhs.start()
     load_walls = pltpu.make_async_copy(walls_in, walls, io.at[4])
     load_walls.start()
     load_stencils = pltpu.make_async_copy(stencils_in, stencils, io.at[5])
     load_stencils.start()
-    for i, lv in enumerate(lvs):
+    load_target = pltpu.make_async_copy(target, stage[0].at[1], io.at[0])
+    load_target.start()
+
+    def clear(i):
+        lv = lvs[i]
         rows = lv.stage_rows * lv.stage_pitch
-        first = rows if i < 2 else 0
-
-        def clear(row, count, i=i):
+
+        def body(row, count):
             stages[i][pl.ds(row, count), :] = jnp.zeros((count, NZ), jnp.float32)
 
-        blocks(first, 2 * rows, clear)
-    load_rhs = pltpu.make_async_copy(rhs, stage[0].at[0], io.at[1])
-    load_rhs.start()
-
-    barrier = pltpu.get_barrier_semaphore()
-    near = [(d, e) for d in (-2, -1, 0, 1, 2) for e in (-1, 0, 1) if (d, e) != (0, 0)]
-    near = sorted(set((d % gx_size, e % gy_size) for d, e in near))
-    for d, e in near:
-        pl.semaphore_signal(barrier, inc=1, device_id=device(gx + d, gy + e), device_id_type=MESH)
-
-    def lay_out(i):
-        lv = lvs[i]
+        blocks((lv.slots - 1) * rows, lv.slots * rows, body)
+
+    def lay_out(lv, mask_to, diag_to):
         wall = [walls[k].astype(jnp.float32) for k in range(6)]
         total_rows, total_cols = gx_size * lv.rows, gy_size * lv.cols
         starts = list(range(0, lv.pitch, 8))
@@ -302,59 +303,37 @@
                 tally = tally + jnp.where(lane == 0, wall[4], 0.0) + jnp.where(lane == NZ - 1, wall[5], 0.0)
                 inside = (column >= 0) & (column < total_cols) & within
                 where = pl.ds(step * lv.pitch + start, 8)
-                diag[i][where, :] = 6.0 - tally
-                mask[i][where, :] = jnp.where(inside, 1.0, 0.0)
+                diag_to[where, :] = 6.0 - tally
+                mask_to[where, :] = jnp.where(inside, 1.0, 0.0)
             return carry
 
         lax.fori_loop(0, lv.high, body, 0)
 
-    def placed(cut, me, size, block):
-        offset, first, count, inward = cut
-        if inward:
-            low = offset > 0
-            swapped = (me == 0) if low else (me == size - 1)
-            step = -1 if low else 1
-            acting = jnp.where(swapped, me + step, me)
-            mirrored = jnp.where(swapped, -offset, offset)
-            other = block - first - count
-            begin = jnp.where(swapped, other + step * block, first)
-            start = jnp.where(swapped, other, first)
-        else:
-            acting, mirrored, begin, start = me, offset, first, first
-        to = acting - mirrored
-        outside = (to < 0) | (to >= size)
-        return begin, to, mirrored * block + start, outside, count
-
-    def exchange(way, i):
-        lv = lvs[i]
-        across = [placed(cut, gx, gx_size, lv.rows) for cut in lv.cuts[0]]
-        along = [placed(cut, gy, gy_size, lv.cols) for cut in lv.cuts[1]]
-        pairs = [(p, q) for p in range(len(across)) for q in range(len(along))]
-        pairs.sort(key=lambda pq: -(hops_x(lv.cuts[0][pq[0]][0]) + hops_y(lv.cuts[1][pq[1]][0])))
-        for p, q in pairs:
-            cut_x, cut_y = lv.cuts[0][p], lv.cuts[1][q]
-            begin_x, to_x, land_x, out_x, count_x = across[p]
-            begin_y, to_y, land_y, out_y, count_y = along[q]
-            dst = blocks3[way][i].at[pl.ds(lv.rim + land_x, count_x), pl.ds(lv.rim + land_y, count_y)]
-            if cut_x[0] == 0 and cut_y[0] == 0:
-                piece = stage[i].at[
-                    0, pl.ds(lv.pad_rows + begin_x, count_x), pl.ds(lv.pad_cols + begin_y, count_y)
-                ]
-                pltpu.make_async_copy(piece, dst, local.at[way, i]).start()
+    def exchange(lv, staged, slot, landing, send_to, recv_to, local_to):
+        rows, cols = lv.cuts
+        pairs = [(x, y) for x in rows for y in cols]
+        pairs.sort(key=lambda pair: -(hops_x(pair[0][0]) + hops_y(pair[1][0])))
+        for (dx, first_x, count_x), (dy, first_y, count_y) in pairs:
+            to_x, to_y = gx - dx, gy - dy
+            window = pl.ds(lv.pad_rows + first_x, count_x), pl.ds(lv.pad_cols + first_y, count_y)
+            dst = landing.at[
+                pl.ds(lv.rim + dx * lv.rows + first_x, count_x), pl.ds(lv.rim + dy * lv.cols + first_y, count_y)
+            ]
+            if dx == 0 and dy == 0:
+                pltpu.make_async_copy(staged.at[slot, window[0], window[1]], dst, local_to).start()
                 continue
-            piece = stage[i].at[
-                jnp.where(out_x | out_y, 1, 0),
-                pl.ds(lv.pad_rows + begin_x, count_x),
-                pl.ds(lv.pad_cols + begin_y, count_y),
-            ]
+            outside = (to_x < 0) | (to_x >= gx_size) | (to_y < 0) | (to_y >= gy_size)
             pltpu.make_async_remote_copy(
-                src_ref=piece,
+                src_ref=staged.at[jnp.where(outside, lv.slots - 1, slot), window[0], window[1]],
                 dst_ref=dst,
-                send_sem=send.at[way, i],
-                recv_sem=recv.at[way, i],
+                send_sem=send_to,
+                recv_sem=recv_to,
                 device_id=device(to_x, to_y),
                 device_id_type=MESH,
             ).start()
+
+    def exchange_level(way, i):
+        exchange(lvs[i], stage[i], 0, blocks3[way][i], send.at[way, i], recv.at[way, i], local.at[way, i])
 
     def await_bytes(ref, rows, sem):
         pltpu.make_async_copy(ref.at[pl.ds(0, rows)], ref.at[pl.ds(0, rows)], sem).wait()
@@ -372,86 +351,121 @@
             return lambda entry: stencils[row, entry]
         return lambda entry: stencils[row, 26 - entry]
 
-    def cycle(way, waiting):
+    def down(way, waiting):
         for i in range(LEVELS):
             lv = lvs[i]
-            exchange(way, i)
+            if i > 0:
+                exchange_level(way, i)
             waiting(i)
-            arrived(way, i)
-            smooth(pre[i], src[way][i], weights(way, i if way == 0 else LEVELS + i), lv, 1, mask[i])
+            if way == 0 or i > 0:
+                arrived(way, i)
+            depth = 2 if (way, i) == (0, 0) else 1
+            smooth(pre[i], src[way][i], weights(way, i if way == 0 else LEVELS + i), lv, depth, mask[i])
             known = max(KNOWN[i + 1])
             remain(mid[i], src[way][i], pre[i], diag[i], mask[i], lv, lv.rim - 2 * known)
-            sent(way, i)
-            if way == 1 and i + 1 == LEVELS:
-                sent(0, LEVELS)
+            if way == 1:
+                sent(0, i + 1)
             restrict(stages[i + 1], mid[i], lv, lvs[i + 1])
-        bottom = lvs[LEVELS]
+
+    def across(way, waiting):
+        lv = lvs[LEVELS]
+        less = way * LESS[LEVELS]
         weight = weights(way, 2 * LEVELS)
-        exchange(way, LEVELS)
+        exchange_level(way, LEVELS)
         waiting(LEVELS)
         arrived(way, LEVELS)
         b = src[way][LEVELS]
         x, y = pre[LEVELS], mid[LEVELS]
         rest = (aft[way][LEVELS], last_rest[way])
-        smooth(x, b, weight, bottom, 1, mask[LEVELS])
-        remain(rest[0], b, x, diag[LEVELS], mask[LEVELS], bottom, 2)
-        smooth(y, rest[0], weight, bottom, 3, mask[LEVELS], x)
-        remain(rest[1], b, y, diag[LEVELS], mask[LEVELS], bottom, 4)
-        smooth(out[LEVELS], rest[1], weight, bottom, 5, mask[LEVELS], y)
-        if way == 1:
-            sent(1, LEVELS)
-        for i in reversed(range(LEVELS)):
+        inside, center = mask[LEVELS], diag[LEVELS]
+        smooth(x, b, weight, lv, 1 + less, inside)
+        remain(rest[0], b, x, center, inside, lv, 2 + less)
+        smooth(y, rest[0], weight, lv, 3 + less, inside, x)
+        remain(rest[1], b, y, center, inside, lv, 4 + less)
+        smooth(out[LEVELS], rest[1], weight, lv, 5 + less, inside, y)
+
+    def up(way):
+        for i in reversed(range(1, LEVELS)):
             lv = lvs[i]
-            prolong_onto(mid[i], pre[i], out[i + 1], lv, lvs[i + 1])
-            remain(aft[way][i], src[way][i], mid[i], diag[i], mask[i], lv, 2)
-            if i > 0:
-                smooth(out[i], aft[way][i], weights(way, LEVELS + i if way == 0 else i), lv, 3, mask[i], mid[i])
-
-    def finish(weight, way, store):
-        lv = lvs[0]
-
-        def body(step, carry):
-            for part in range(UNROLL):
-                line = step * UNROLL + part
-                row = (lv.rim + line) * lv.pitch + lv.rim
-                value = stencil_at(aft[way][0], weight, lv.pitch, row, lv.cols)
-                store(line, value + mid[0][pl.ds(row, lv.cols), :])
-            return carry
-
-        lax.fori_loop(0, lv.rows // UNROLL, body, 0)
-
+            less = way * LESS[i]
+            prolong_onto(mid[i], pre[i], out[i + 1], lv, lvs[i + 1], 3 - way)
+            remain(aft[way][i], src[way][i], mid[i], diag[i], mask[i], lv, 2 + less)
+            weight = weights(way, LEVELS + i if way == 0 else i)
+            smooth(out[i], aft[way][i], weight, lv, 3 + less, mask[i], mid[i])
+
+    fine = lvs[0]
     load_walls.wait()
-    lay_out(0)
+    lay_out(fine, mask[0], diag[0])
+    clear(0)
     load_stencils.wait()
     load_rhs.wait()
     pl.semaphore_wait(barrier, len(near))
+    exchange_level(0, 0)
+    load_target.wait()
+    exchange(wide, stage[0], 0, grid3(wide_src, wide), extra_send.at[0], extra_recv.at[0], extra_local.at[0])
+    exchange(fine, stage[0], 1, grid3(goal, fine), extra_send.at[1], extra_recv.at[1], extra_local.at[1])
 
     def forward_waits(i):
         if i == 0:
+            sums[...] = jnp.zeros(sums.shape, jnp.float32)
             for level in range(1, LEVELS + 1):
-                lay_out(level)
-            rows = sums.shape[0]
-            sums[...] = jnp.zeros((rows, NZ), jnp.float32)
-
-    cycle(0, forward_waits)
-
-    load_target.wait()
-
-    def store_solution(step, value):
-        result[step] = value
-        stage[0][0, step] = value - goal[step]
-
-    finish(weights(0, LEVELS), 0, store_solution)
-    save_solution = pltpu.make_async_copy(result, solution_out, io.at[2])
+                clear(level)
+                lay_out(lvs[level], mask[level], diag[level])
+        if i == 1:
+            lay_out(wide, wide_mask, wide_diag)
+        if i == 2:
+            await_bytes(wide_src, wide.arriving, extra_recv.at[0])
+            await_bytes(wide_src, wide.high * wide.pitch - wide.arriving, extra_local.at[0])
+            smooth(wide_pre, wide_src, weights(0, 0), wide, 1, wide_mask)
+        if i == LEVELS:
+            await_bytes(goal, fine.arriving, extra_recv.at[1])
+            await_bytes(goal, fine.high * fine.pitch - fine.arriving, extra_local.at[1])
+            await_bytes(wide_src, wide.arriving, extra_send.at[0])
+            await_bytes(goal, fine.arriving, extra_send.at[1])
+            sent(0, 0)
+
+    down(0, forward_waits)
+    across(0, forward_waits)
+    up(0)
+    prolong_onto(wide_mid, wide_pre, out[1], wide, lvs[1], 3)
+    remain(wide_aft, wide_src, wide_mid, wide_diag, wide_mask, wide, 2)
+    smooth(wide_out, wide_aft, weights(0, LEVELS), wide, 3, wide_mask, wide_mid)
+
+    pitch8 = -(-fine.pitch // 8) * 8
+    inset = wide.rim - fine.rim
+
+    def error_at(step, carry):
+        for part in range(fine.high // 2):
+            line = step * (fine.high // 2) + part
+            where = pl.ds(line * fine.pitch, pitch8)
+            src[1][0][where, :] = wide_out[pl.ds((line + inset) * wide.pitch + inset, pitch8), :] - goal[where, :]
+        return carry
+
+    lax.fori_loop(0, 2, error_at, 0)
+    own_solution = grid3(wide_out, wide).at[pl.ds(wide.rim, fine.rows), pl.ds(wide.rim, fine.cols)]
+    save_solution = pltpu.make_async_copy(own_solution, solution_out, io.at[2])
     save_solution.start()
 
+    def post_sums(i):
+        field = aft[0][i] if i else wide_aft
+        lv = lvs[i] if i else wide
+        if i:
+            cot, first, pitch = stages[i], lvs[i].pad_rows * lvs[i].stage_pitch + lvs[i].pad_cols, lvs[i].stage_pitch
+        else:
+            cot, first, pitch = src[1][0], fine.rim * fine.pitch + fine.rim, fine.pitch
+        keep_sums(sums, products(cot, first, pitch, field, lv), LEVELS + i)
+
     def backward_waits(i):
-        lv = lvs[i]
-        if i < LEVELS:
-            first = lv.pad_rows * lv.stage_pitch + lv.pad_cols
-            keep_sums(sums, products(stages[i], first, lv.stage_pitch, aft[0][i], lv), LEVELS + i)
-
-    cycle(1, backward_waits)
+        if i == 1:
+            post_sums(0)
+        if 1 <= i < LEVELS:
+            post_sums(i)
+
+    down(1, backward_waits)
+    across(1, backward_waits)
+    up(1)
+    prolong_onto(mid[0], pre[0], out[1], fine, lvs[1], 1)
+    remain(aft[1][0], src[1][0], mid[0], diag[0], mask[0], fine, 2)
 
     bottom = lvs[LEVELS]
     at = bottom.rim * bottom.pitch + bottom.rim
@@ -498,10 +512,15 @@
     order = sorted(range(1, gy_size), key=lambda step: -min(step, gy_size - step))
     spread(0, over_y, gy, order, lambda step: device(gx, gy + step))
 
-    def store_grad(step, value):
-        grad[step] = value
-
-    finish(weights(1, 0), 1, store_grad)
+    def grad_at(step, carry):
+        for part in range(UNROLL):
+            line = step * UNROLL + part
+            row = (fine.rim + line) * fine.pitch + fine.rim
+            value = stencil_at(aft[1][0], weights(1, 0), fine.pitch, row, fine.cols)
+            grad[line] = value + mid[0][pl.ds(row, fine.cols), :]
+        return carry
+
+    lax.fori_loop(0, fine.rows // UNROLL, grad_at, 0)
     save_grad = pltpu.make_async_copy(grad, grad_out, io.at[3])
     save_grad.start()
 
@@ -509,6 +528,8 @@
     order = sorted(range(1, gx_size), key=lambda step: -min(step % 8, 8 - step % 8) - min(step, gx_size - step) / 8)
     spread(1, over_x, gx, order, lambda step: device(gx + step, gy))
     await_bytes(src[0][0], 3 * (gy_size - 1), reduce_send.at[0])
+    for i in range(1, LEVELS + 1):
+        sent(1, i)
     save_solution.wait()
     save_grad.wait()
     total = gathered(1, over_x, gx_size)
@@ -520,16 +541,27 @@
         weights_out[pl.ds(row, 1), :] = total[part : part + 1, lane : lane + 27] * scale
 
 
+def put_out(*refs):
+    sems = refs[6]
+    copies = [pltpu.make_async_copy(refs[i], refs[3 + i], sems.at[i]) for i in range(3)]
+    for copy in copies:
+        copy.start()
+    for copy in copies:
+        copy.wait()
+
+
 def on_device(gx_size, gy_size, rhs, target, stencils, face_mask):
     rows, cols, _ = rhs.shape
-    lvs = [Level(i, (rows >> i, cols >> i)) for i in range(LEVELS + 1)]
+    lvs = [Level(i, (rows >> i, cols >> i), RIM[i]) for i in range(LEVELS + 1)]
+    wide = Level(0, (rows, cols), WIDE)
     field = lambda lv: pltpu.VMEM((lv.store * lv.pitch, NZ), jnp.float32)
     scratch = []
     for _ in range(9):
         scratch += [field(lv) for lv in lvs]
-    scratch += [pltpu.VMEM((2, lv.stage_rows, lv.stage_pitch, NZ), jnp.float32) for lv in lvs]
+    scratch += [pltpu.VMEM((lv.slots, lv.stage_rows, lv.stage_pitch, NZ), jnp.float32) for lv in lvs]
     scratch += [field(lvs[LEVELS])] * 2
-    scratch += [pltpu.VMEM((rows, cols, NZ), jnp.float32)] * 3
+    scratch += [field(wide)] * 7
+    scratch += [field(lvs[0]), pltpu.VMEM((rows, cols, NZ), jnp.float32)]
     scratch += [
         pltpu.VMEM((3 * NZ, NZ), jnp.float32),
         pltpu.VMEM((2, 8, NZ), jnp.float32),
@@ -543,9 +575,12 @@
         pltpu.SemaphoreType.DMA((6,)),
         pltpu.SemaphoreType.DMA((2,)),
         pltpu.SemaphoreType.DMA((2,)),
+        pltpu.SemaphoreType.DMA((2,)),
+        pltpu.SemaphoreType.DMA((2,)),
+        pltpu.SemaphoreType.DMA((2,)),
     ]
-    return pl.pallas_call(
-        functools.partial(kernel, gx_size, gy_size, lvs),
+    results = pl.pallas_call(
+        functools.partial(kernel, gx_size, gy_size, lvs + [wide]),
         out_shape=(
             jax.ShapeDtypeStruct(rhs.shape, jnp.float32),
             jax.ShapeDtypeStruct(rhs.shape, jnp.float32),
@@ -568,6 +603,14 @@
         ),
         cost_estimate=pl.CostEstimate(flops=60_000_000, bytes_accessed=1_100_000, transcendentals=0),
     )(rhs, target, stencils, face_mask)
+    return pl.pallas_call(
+        put_out,
+        out_shape=tuple(jax.ShapeDtypeStruct(r.shape, r.dtype) for r in results),
+        in_specs=[pl.BlockSpec(memory_space=pl.ANY)] * 3,
+        out_specs=(pl.BlockSpec(memory_space=pl.ANY),) * 3,
+        scratch_shapes=[pltpu.SemaphoreType.DMA((3,))],
+        compiler_params=pltpu.CompilerParams(vmem_limit_bytes=60 << 20),
+    )(*results)
 
 
 def solution(mesh):

time: 89.4 us -> 105 us (1.17)
  Pallas kernels: 85.5 us -> 104 us
  local copies, waits for them, and re-layouts: 3.02 us -> 0 us
    pallas_call x1 -> x2, Pallas kernels: 85.5 us -> 104 us  [the longest x1 87.1 us: on_device(): pl.pallas_call(functools.partial(kernel, gx_size, gy_size, lvs + [wide]),...]
    unnamed x7 -> x0, local copies, waits for them, and re-layouts: 3.02 us -> none
where the time goes in v3:
time: 105 us
  Pallas kernels  104 us (99%)
    pallas_call x1, Pallas kernels, on_device(): pl.pallas_call(functools.partial(kernel, gx_size, gy_size, lvs + [wide]),...  87.1 us
    pallas_call x1, Pallas kernels, on_device(): pl.pallas_call(put_out, out_shape=tuple((jax.ShapeDtypeStruct(r.shape, r....  17.2 us

profile of v3, /device:TPU:1, one launch (start us, length us, event | category | flops | bytes accessed | tf_op | source)
XLA Modules:
  0.0 104.9 jit_solution(567128763265046516)
XLA Ops:
  0.6 87.1 %shard_map.67 = (f32[16,32,128]{2,1,0:T(8,128)}, f32[16,32,128]{2,1,0:T(8,128)}, f32[9,27]{1,0:T(8,128)}) custom-call(f32[16,32,128]{2,1,0:T(8,128)} %rhs.1, f32[16,32,128]{2,1,0:T(8,128)} %target.1, f32[9,27]{1,0:T(8,128)} %stencils_in.1, s32[6]{0:T(128)} %walls_in.1), custom_call_target="tpu_custom_call" | custom-call | flops 60000000 | bytes 1100000 | tf_op jit(solution)/shard_map/pallas_call | solution.py:582
  87.7 17.2 %shard_map.68 = (f32[16,32,128]{2,1,0:T(8,128)}, f32[16,32,128]{2,1,0:T(8,128)}, f32[9,27]{1,0:T(8,128)}) custom-call(f32[16,32,128]{2,1,0:T(8,128)} %get-tuple-element.6.refs_0_, f32[16,32,128]{2,1,0:T(8,128)} %get-tuple-element.7.refs_1_, f32[9,27]{1,0:T(8,128)} %get-tuple-element.8.refs_2_), custom_call_target="tpu_custom_call" | custom-call | tf_op jit(solution)/shard_map/pallas_call | solution.py:606

commit v4 on v3

--- a/solution.py
+++ b/solution.py
@@ -152,11 +152,8 @@
         return carry
 
     count = below.rows + 2 * known_rows
-    if count <= 4:
-        for step in range(count):
-            body(step, 0)
-    else:
-        lax.fori_loop(0, count, body, 0)
+    for step in range(count):
+        body(step, 0)
 
 
 def prolong_onto(dst, base, coarse, lv, below, half):
@@ -183,8 +180,8 @@
                     dst[where, :] = base[where, :] + value
         return carry
 
-    count = below.rows + 2 * half
-    lax.fori_loop(0, count, body, 0)
+    for step in range(below.rows + 2 * half):
+        body(step, 0)
 
 
 def folded(v):
@@ -394,17 +391,14 @@
             smooth(out[i], aft[way][i], weight, lv, 3 + less, mask[i], mid[i])
 
     fine = lvs[0]
-    load_walls.wait()
-    lay_out(fine, mask[0], diag[0])
     clear(0)
-    load_stencils.wait()
     load_rhs.wait()
     pl.semaphore_wait(barrier, len(near))
     exchange_level(0, 0)
+    load_walls.wait()
+    load_stencils.wait()
+    lay_out(fine, mask[0], diag[0])
     load_target.wait()
-    exchange(wide, stage[0], 0, grid3(wide_src, wide), extra_send.at[0], extra_recv.at[0], extra_local.at[0])
-    exchange(fine, stage[0], 1, grid3(goal, fine), extra_send.at[1], extra_recv.at[1], extra_local.at[1])
-
     def forward_waits(i):
         if i == 0:
             sums[...] = jnp.zeros(sums.shape, jnp.float32)
@@ -412,8 +406,11 @@
                 clear(level)
                 lay_out(lvs[level], mask[level], diag[level])
         if i == 1:
+            exchange(wide, stage[0], 0, grid3(wide_src, wide), extra_send.at[0], extra_recv.at[0], extra_local.at[0])
             lay_out(wide, wide_mask, wide_diag)
         if i == 2:
+            exchange(fine, stage[0], 1, grid3(goal, fine), extra_send.at[1], extra_recv.at[1], extra_local.at[1])
+        if i == 3:
             await_bytes(wide_src, wide.arriving, extra_recv.at[0])
             await_bytes(wide_src, wide.high * wide.pitch - wide.arriving, extra_local.at[0])
             smooth(wide_pre, wide_src, weights(0, 0), wide, 1, wide_mask)
@@ -542,12 +539,16 @@
 
 
 def put_out(*refs):
-    sems = refs[6]
-    copies = [pltpu.make_async_copy(refs[i], refs[3 + i], sems.at[i]) for i in range(3)]
-    for copy in copies:
-        copy.start()
-    for copy in copies:
-        copy.wait()
+    sources, targets, held, sems = refs[:3], refs[3:6], refs[6:9], refs[9]
+    loads = [pltpu.make_async_copy(sources[i], held[i], sems.at[0, i]) for i in range(3)]
+    stores = [pltpu.make_async_copy(held[i], targets[i], sems.at[1, i]) for i in range(3)]
+    for load in loads:
+        load.start()
+    for load, store in zip(loads, stores):
+        load.wait()
+        store.start()
+    for store in stores:
+        store.wait()
 
 
 def on_device(gx_size, gy_size, rhs, target, stencils, face_mask):
@@ -608,7 +609,7 @@
         out_shape=tuple(jax.ShapeDtypeStruct(r.shape, r.dtype) for r in results),
         in_specs=[pl.BlockSpec(memory_space=pl.ANY)] * 3,
         out_specs=(pl.BlockSpec(memory_space=pl.ANY),) * 3,
-        scratch_shapes=[pltpu.SemaphoreType.DMA((3,))],
+        scratch_shapes=[pltpu.VMEM(r.shape, r.dtype) for r in results] + [pltpu.SemaphoreType.DMA((2, 3))],
         compiler_params=pltpu.CompilerParams(vmem_limit_bytes=60 << 20),
     )(*results)
 

time: 105 us -> 89.1 us (0.85)
  Pallas kernels: 104 us -> 88.2 us
    pallas_call x1, Pallas kernels: 17.2 us -> 1.79 us  [on_device(): pl.pallas_call(put_out, out_shape=tuple((jax.ShapeDtypeStruct(r.shape, r....]
where the time goes in v4:
time: 89.1 us; the launch traced here: 89 us
  Pallas kernels  88.2 us (99%)
    pallas_call x1, Pallas kernels, on_device(): pl.pallas_call(functools.partial(kernel, gx_size, gy_size, lvs + [wide]),...  86.4 us
    pallas_call x1, Pallas kernels, on_device(): pl.pallas_call(put_out, out_shape=tuple((jax.ShapeDtypeStruct(r.shape, r....  1.79 us

profile of v4, /device:TPU:1, one launch (start us, length us, event | category | flops | bytes accessed | tf_op | source)
XLA Modules:
  0.0 89.0 jit_solution(3630359428058242322)
XLA Ops:
  0.6 86.4 %shard_map.67 = (f32[16,32,128]{2,1,0:T(8,128)}, f32[16,32,128]{2,1,0:T(8,128)}, f32[9,27]{1,0:T(8,128)}) custom-call(f32[16,32,128]{2,1,0:T(8,128)} %rhs.1, f32[16,32,128]{2,1,0:T(8,128)} %target.1, f32[9,27]{1,0:T(8,128)} %stencils_in.1, s32[6]{0:T(128)} %walls_in.1), custom_call_target="tpu_custom_call" | custom-call | flops 60000000 | bytes 1100000 | tf_op jit(solution)/shard_map/pallas_call | solution.py:583
  87.0 1.8 %shard_map.68 = (f32[16,32,128]{2,1,0:T(8,128)}, f32[16,32,128]{2,1,0:T(8,128)}, f32[9,27]{1,0:T(8,128)}) custom-call(f32[16,32,128]{2,1,0:T(8,128)} %get-tuple-element.6.refs_0_, f32[16,32,128]{2,1,0:T(8,128)} %get-tuple-element.7.refs_1_, f32[9,27]{1,0:T(8,128)} %get-tuple-element.8.refs_2_), custom_call_target="tpu_custom_call" | custom-call | tf_op jit(solution)/shard_map/pallas_call | solution.py:607

commit v5 on v2

--- a/solution.py
+++ b/solution.py
@@ -151,11 +151,8 @@
         return carry
 
     count = below.rows + 2 * known_rows
-    if count <= 4:
-        for step in range(count):
-            body(step, 0)
-    else:
-        lax.fori_loop(0, count, body, 0)
+    for step in range(count):
+        body(step, 0)
 
 
 def prolong_onto(dst, base, coarse, lv, below):
@@ -183,8 +180,8 @@
                     dst[where, :] = base[where, :] + value
         return carry
 
-    count = below.rows + 2 * half
-    lax.fori_loop(0, count, body, 0)
+    for step in range(below.rows + 2 * half):
+        body(step, 0)
 
 
 def folded(v):
@@ -262,6 +259,14 @@
     def device(x, y):
         return (lax.rem(x + 2 * gx_size, gx_size), lax.rem(y + 2 * gy_size, gy_size))
 
+    barrier = pltpu.get_barrier_semaphore()
+    near = [(d, e) for d in (-2, -1, 0, 1, 2) for e in (-1, 0, 1) if (d, e) != (0, 0)]
+    near = sorted(set((d % gx_size, e % gy_size) for d, e in near))
+    for d, e in near:
+        pl.semaphore_signal(barrier, inc=1, device_id=device(gx + d, gy + e), device_id_type=MESH)
+
+    load_rhs = pltpu.make_async_copy(rhs, stage[0].at[0], io.at[1])
+    load_rhs.start()
     load_target = pltpu.make_async_copy(target, goal, io.at[0])
     load_target.start()
     load_walls = pltpu.make_async_copy(walls_in, walls, io.at[4])
@@ -276,14 +281,6 @@
             stages[i][pl.ds(row, count), :] = jnp.zeros((count, NZ), jnp.float32)
 
         blocks(first, 2 * rows, clear)
-    load_rhs = pltpu.make_async_copy(rhs, stage[0].at[0], io.at[1])
-    load_rhs.start()
-
-    barrier = pltpu.get_barrier_semaphore()
-    near = [(d, e) for d in (-2, -1, 0, 1, 2) for e in (-1, 0, 1) if (d, e) != (0, 0)]
-    near = sorted(set((d % gx_size, e % gy_size) for d, e in near))
-    for d, e in near:
-        pl.semaphore_signal(barrier, inc=1, device_id=device(gx + d, gy + e), device_id_type=MESH)
 
     def lay_out(i):
         lv = lvs[i]
@@ -421,14 +418,13 @@
         lax.fori_loop(0, lv.rows // UNROLL, body, 0)
 
     load_walls.wait()
-    lay_out(0)
     load_stencils.wait()
     load_rhs.wait()
     pl.semaphore_wait(barrier, len(near))
 
     def forward_waits(i):
         if i == 0:
-            for level in range(1, LEVELS + 1):
+            for level in range(LEVELS + 1):
                 lay_out(level)
             rows = sums.shape[0]
             sums[...] = jnp.zeros((rows, NZ), jnp.float32)
@@ -518,6 +514,19 @@
         scale = SCALES[row % LEVELS if row < 2 * LEVELS else LEVELS] / cells
         part, lane = row // 4, 32 * (row % 4)
         weights_out[pl.ds(row, 1), :] = total[part : part + 1, lane : lane + 27] * scale
+
+
+def put_out(*refs):
+    sources, targets, held, sems = refs[:3], refs[3:6], refs[6:9], refs[9]
+    loads = [pltpu.make_async_copy(sources[i], held[i], sems.at[0, i]) for i in range(3)]
+    stores = [pltpu.make_async_copy(held[i], targets[i], sems.at[1, i]) for i in range(3)]
+    for load in loads:
+        load.start()
+    for load, store in zip(loads, stores):
+        load.wait()
+        store.start()
+    for store in stores:
+        store.wait()
 
 
 def on_device(gx_size, gy_size, rhs, target, stencils, face_mask):
@@ -544,7 +553,7 @@
         pltpu.SemaphoreType.DMA((2,)),
         pltpu.SemaphoreType.DMA((2,)),
     ]
-    return pl.pallas_call(
+    results = pl.pallas_call(
         functools.partial(kernel, gx_size, gy_size, lvs),
         out_shape=(
             jax.ShapeDtypeStruct(rhs.shape, jnp.float32),
@@ -568,6 +577,14 @@
         ),
         cost_estimate=pl.CostEstimate(flops=60_000_000, bytes_accessed=1_100_000, transcendentals=0),
     )(rhs, target, stencils, face_mask)
+    return pl.pallas_call(
+        put_out,
+        out_shape=tuple(jax.ShapeDtypeStruct(r.shape, r.dtype) for r in results),
+        in_specs=[pl.BlockSpec(memory_space=pl.ANY)] * 3,
+        out_specs=(pl.BlockSpec(memory_space=pl.ANY),) * 3,
+        scratch_shapes=[pltpu.VMEM(r.shape, r.dtype) for r in results] + [pltpu.SemaphoreType.DMA((2, 3))],
+        compiler_params=pltpu.CompilerParams(vmem_limit_bytes=60 << 20),
+    )(*results)
 
 
 def solution(mesh):

time: 89.4 us -> 87.5 us (0.979)
  local copies, waits for them, and re-layouts: 3.02 us -> 0 us
  Pallas kernels: 85.5 us -> 86.7 us
    unnamed x7 -> x0, local copies, waits for them, and re-layouts: 3.02 us -> none
    pallas_call x0 -> x1, Pallas kernels: none -> 1.79 us  [on_device(): pl.pallas_call(put_out, out_shape=tuple((jax.ShapeDtypeStruct(r.shape, r....]
where the time goes in v5:
time: 87.5 us; the launch traced here: 87.3 us
  Pallas kernels  86.7 us (99%)
    pallas_call x1, Pallas kernels, on_device(): pl.pallas_call(functools.partial(kernel, gx_size, gy_size, lvs), out_shap...  84.9 us
    pallas_call x1, Pallas kernels, on_device(): pl.pallas_call(put_out, out_shape=tuple((jax.ShapeDtypeStruct(r.shape, r....  1.79 us

profile of v5, /device:TPU:1, one launch (start us, length us, event | category | flops | bytes accessed | tf_op | source)
XLA Modules:
  0.0 87.3 jit_solution(9741112302359892378)
XLA Ops:
  0.6 84.9 %shard_map.67 = (f32[16,32,128]{2,1,0:T(8,128)}, f32[16,32,128]{2,1,0:T(8,128)}, f32[9,27]{1,0:T(8,128)}) custom-call(f32[16,32,128]{2,1,0:T(8,128)} %rhs.1, f32[16,32,128]{2,1,0:T(8,128)} %target.1, f32[9,27]{1,0:T(8,128)} %stencils_in.1, s32[6]{0:T(128)} %walls_in.1), custom_call_target="tpu_custom_call" | custom-call | flops 60000000 | bytes 1100000 | tf_op jit(solution)/shard_map/pallas_call | solution.py:556
  85.5 1.8 %shard_map.68 = (f32[16,32,128]{2,1,0:T(8,128)}, f32[16,32,128]{2,1,0:T(8,128)}, f32[9,27]{1,0:T(8,128)}) custom-call(f32[16,32,128]{2,1,0:T(8,128)} %get-tuple-element.6.refs_0_, f32[16,32,128]{2,1,0:T(8,128)} %get-tuple-element.7.refs_1_, f32[9,27]{1,0:T(8,128)} %get-tuple-element.8.refs_2_), custom_call_target="tpu_custom_call" | custom-call | tf_op jit(solution)/shard_map/pallas_call | solution.py:580

commit v6 on v5

--- a/solution.py
+++ b/solution.py
@@ -10,7 +10,7 @@
 MESH = pl.DeviceIdType.MESH
 LEVELS = 4
 NZ = 128
-CHUNK = 384
+CHUNK = 1024
 UNROLL = 8
 RIM = (3, 4, 5, 5, 7)
 KNOWN = ((0, 0), (0, 0), (1, 0), (1, 1), (1, 1))

time: 87.5 us -> 87.4 us (level)
  no operation moved by 1% of the time
where the time goes in v6:
time: 87.4 us; the launch traced here: 87.2 us
  Pallas kernels  86.6 us (99%)
    pallas_call x1, Pallas kernels, on_device(): pl.pallas_call(functools.partial(kernel, gx_size, gy_size, lvs), out_shap...  84.8 us
    pallas_call x1, Pallas kernels, on_device(): pl.pallas_call(put_out, out_shape=tuple((jax.ShapeDtypeStruct(r.shape, r....  1.79 us

profile of v6, /device:TPU:1, one launch (start us, length us, event | category | flops | bytes accessed | tf_op | source)
XLA Modules:
  0.0 87.2 jit_solution(3015381335491109799)
XLA Ops:
  0.6 84.8 %shard_map.67 = (f32[16,32,128]{2,1,0:T(8,128)}, f32[16,32,128]{2,1,0:T(8,128)}, f32[9,27]{1,0:T(8,128)}) custom-call(f32[16,32,128]{2,1,0:T(8,128)} %rhs.1, f32[16,32,128]{2,1,0:T(8,128)} %target.1, f32[9,27]{1,0:T(8,128)} %stencils_in.1, s32[6]{0:T(128)} %walls_in.1), custom_call_target="tpu_custom_call" | custom-call | flops 60000000 | bytes 1100000 | tf_op jit(solution)/shard_map/pallas_call | solution.py:556
  85.4 1.8 %shard_map.68 = (f32[16,32,128]{2,1,0:T(8,128)}, f32[16,32,128]{2,1,0:T(8,128)}, f32[9,27]{1,0:T(8,128)}) custom-call(f32[16,32,128]{2,1,0:T(8,128)} %get-tuple-element.6.refs_0_, f32[16,32,128]{2,1,0:T(8,128)} %get-tuple-element.7.refs_1_, f32[9,27]{1,0:T(8,128)} %get-tuple-element.8.refs_2_), custom_call_target="tpu_custom_call" | custom-call | tf_op jit(solution)/shard_map/pallas_call | solution.py:580
